TPU v7x, 256 devices: a whole 4x4x8 slice. The times are simulated.
256 devices in a mesh: req: 16 (over y, x), lend: 16 (over z, core).
Axes of the slice: x: 4, y: 4, z: 8, core: 2. Of those that a mesh axis runs over, the one named last changes fastest.
Arguments:
- queries: bfloat16 [4, 256, 4096], P(None, ('req', 'lend')), may hold values from -150 to 150
- new_keys: bfloat16 [4, 256, 512], P(None, ('req', 'lend')), may hold values from -6 to 6
- new_values: bfloat16 [4, 256, 512], P(None, ('req', 'lend')), may hold values from -6 to 6
- key_pool: bfloat16 [12288, 128, 512], P(('req', 'lend')), may hold values from -6 to 6
- value_pool: bfloat16 [12288, 128, 512], P(('req', 'lend')), may hold values from -6 to 6
- key_scale: float32 [12288, 16, 128], P(('req', 'lend')), may hold values from 0.25 to 4
- value_scale: float32 [12288, 16, 128], P(('req', 'lend')), may hold values from 0.25 to 4
- page_request: int32 [12288], P(('req', 'lend')), may hold values from 0 to 255, as said below
- page_fill: int32 [12288], P(('req', 'lend')), may hold values from 0 to 128, as said below
- sinks: float32 [64], replicated, may hold values from 3 to 9
Outputs:
- attended: bfloat16 [4, 256, 4096], P(None, ('req', 'lend'))
Inputs may be any that keep to these rules, and one draw needn't show every extreme that they name: `page_request`: A page slot on the device at flat index d = r * 16 + l (r its req index, l its lend index) holds tokens of a request owned by a device with req index r or with lend index l; request i is owned by flat device i. Some requests own far more pages than others. `page_fill`: free slots have 0. On each device the slots in use come first; every device uses three quarters or more of its 48 slots, and some device uses all of them.
All inputs are finite; a program needn't handle non-finite values.
Results may differ from a plain program's by a relative error of at most 0.0055.
The roundings to bfloat16 on the way count: a program that leaves them out, or rounds other values in their place, can miss the bound.
Values may be sent and summed in bfloat16 or wider, within the bound.
A program may use at most 128 MiB of HBM per device.

v0:
```python
import jax
import jax.numpy as jnp
from jax import lax
from jax.sharding import PartitionSpec as P

FLOOR = -1e30
SCORE_SCALE = 0.125


def dequantize(pool, scales):
    pages, tokens, width = pool.shape
    blocks = scales.shape[1]
    spread = jnp.swapaxes(scales, 1, 2)[..., None]
    shaped = pool.astype(jnp.float32).reshape(pages, tokens, blocks, width // blocks)
    return (shaped * spread).reshape(pages, tokens, width).astype(jnp.bfloat16)


def page_terms(page_query, keys_deq, values_deq, fills, heads, kv_heads):
    steps, pages, qwidth = page_query.shape
    tokens = keys_deq.shape[1]
    head_size = qwidth // heads
    per_group = heads // kv_heads
    query_heads = page_query.reshape(steps, pages, kv_heads, per_group, head_size)
    key_heads = keys_deq.reshape(pages, tokens, kv_heads, head_size)
    value_heads = values_deq.reshape(pages, tokens, kv_heads, head_size)
    scores = (
        jnp.einsum("spgae,ptge->spgat", query_heads, key_heads, preferred_element_type=jnp.float32)
        * SCORE_SCALE
    )
    valid = (jnp.arange(tokens)[None, :] < fills[:, None])[None, :, None, None, :]
    scores = jnp.where(valid, scores, FLOOR)
    top = jnp.max(scores, axis=-1)
    weights = jnp.where(valid, jnp.exp(scores - top[..., None]), 0.0)
    total = jnp.sum(weights, axis=-1)
    numer = jnp.einsum(
        "spgat,ptge->spgae",
        weights.astype(jnp.bfloat16),
        value_heads,
        preferred_element_type=jnp.float32,
    )
    return (
        top.reshape(steps, pages, heads),
        total.reshape(steps, pages, heads),
        numer.reshape(steps, pages, heads, head_size),
    )


def gather_slots(top, total, numer, slot, count):
    page_top = jnp.moveaxis(top, 1, 0)
    page_total = jnp.moveaxis(total, 1, 0)
    page_numer = jnp.moveaxis(numer, 1, 0)
    best = jnp.maximum(jax.ops.segment_max(page_top, slot, num_segments=count), FLOOR)
    factor = jnp.exp(page_top - best[slot])
    summed = jax.ops.segment_sum(page_total * factor, slot, num_segments=count)
    weighted = jax.ops.segment_sum(page_numer * factor[..., None], slot, num_segments=count)
    return (best, summed, weighted)


def combine_sources(best, summed, weighted):
    highest = jnp.max(best, axis=0)
    factor = jnp.exp(best - highest[None])
    return (
        highest,
        jnp.sum(summed * factor, axis=0),
        jnp.sum(weighted * factor[..., None], axis=0),
    )


def finalize(best, total, numer, queries, new_keys, new_values, sinks, heads, kv_heads):
    steps, rows, qwidth = queries.shape
    head_size = qwidth // heads
    per_group = heads // kv_heads
    query_heads = queries.reshape(steps, rows, kv_heads, per_group, head_size)
    fresh_keys = new_keys.reshape(steps, rows, kv_heads, head_size)
    fresh_values = new_values.reshape(steps, rows, kv_heads, head_size)
    fresh = (
        jnp.einsum("srgae,urge->srgau", query_heads, fresh_keys, preferred_element_type=jnp.float32)
        * SCORE_SCALE
    )
    causal = (jnp.arange(steps)[None, :] <= jnp.arange(steps)[:, None])[:, None, None, None, :]
    fresh = jnp.where(causal, fresh, FLOOR)
    cached = jnp.transpose(best, (1, 0, 2)).reshape(steps, rows, kv_heads, per_group)
    cached_total = jnp.transpose(total, (1, 0, 2)).reshape(steps, rows, kv_heads, per_group)
    cached_numer = jnp.transpose(numer, (1, 0, 2, 3)).reshape(
        steps, rows, kv_heads, per_group, head_size
    )
    sink_logit = sinks.reshape(kv_heads, per_group)
    highest = jnp.maximum(jnp.maximum(cached, jnp.max(fresh, axis=-1)), sink_logit)
    keep = jnp.exp(cached - highest)
    weights = jnp.where(causal, jnp.exp(fresh - highest[..., None]), 0.0)
    denom = cached_total * keep + jnp.sum(weights, axis=-1) + jnp.exp(sink_logit - highest)
    result = cached_numer * keep[..., None] + jnp.einsum(
        "srgau,urge->srgae",
        weights.astype(jnp.bfloat16),
        fresh_values,
        preferred_element_type=jnp.float32,
    )
    return (result / denom[..., None]).reshape(steps, rows, qwidth).astype(jnp.bfloat16)


def on_device(
    queries,
    new_keys,
    new_values,
    key_pool,
    value_pool,
    key_scale,
    value_scale,
    page_request,
    page_fill,
    sinks,
):
    steps, owned, qwidth = queries.shape
    heads = sinks.shape[0]
    head_size = qwidth // heads
    kv_heads = key_pool.shape[2] // head_size
    lend_count = lax.axis_size("lend")
    req_count = lax.axis_size("req")
    req_here = lax.axis_index("req")
    owner = page_request // owned
    member = page_request % owned
    owner_req = owner // lend_count
    owner_lend = owner % lend_count
    slot = jnp.where(
        owner_req == req_here,
        owner_lend * owned + member,
        (lend_count + owner_req) * owned + member,
    )
    row_slots = lend_count * owned
    count = (lend_count + req_count) * owned
    keys_deq = dequantize(key_pool, key_scale)
    values_deq = dequantize(value_pool, value_scale)

    def lent_partials(query_block):
        row_query = lax.all_gather(query_block, "lend", axis=1, tiled=True)
        column_query = lax.all_gather(query_block, "req", axis=1, tiled=True)
        candidates = jnp.concatenate([row_query, column_query], axis=1)
        page_query = jnp.take(candidates, slot, axis=1)
        top, total, numer = page_terms(page_query, keys_deq, values_deq, page_fill, heads, kv_heads)
        best, summed, weighted = gather_slots(top, total, numer, slot, count)
        span = best.shape[1]
        row_best, row_sum, row_weighted = (
            lax.all_to_all(best[:row_slots], "lend", split_axis=0, concat_axis=0, tiled=True),
            lax.all_to_all(summed[:row_slots], "lend", split_axis=0, concat_axis=0, tiled=True),
            lax.all_to_all(weighted[:row_slots], "lend", split_axis=0, concat_axis=0, tiled=True),
        )
        col_best, col_sum, col_weighted = (
            lax.all_to_all(best[row_slots:], "req", split_axis=0, concat_axis=0, tiled=True),
            lax.all_to_all(summed[row_slots:], "req", split_axis=0, concat_axis=0, tiled=True),
            lax.all_to_all(weighted[row_slots:], "req", split_axis=0, concat_axis=0, tiled=True),
        )
        sources = lend_count + req_count
        all_best = jnp.concatenate([row_best, col_best], axis=0).reshape(
            sources, owned, span, heads
        )
        all_sum = jnp.concatenate([row_sum, col_sum], axis=0).reshape(sources, owned, span, heads)
        all_weighted = jnp.concatenate([row_weighted, col_weighted], axis=0).reshape(
            sources, owned, span, heads, head_size
        )
        return combine_sources(all_best, all_sum, all_weighted)

    pieces = [lent_partials(queries[index : index + 1]) for index in range(steps)]
    best = jnp.concatenate([piece[0] for piece in pieces], axis=1)
    summed = jnp.concatenate([piece[1] for piece in pieces], axis=1)
    weighted = jnp.concatenate([piece[2] for piece in pieces], axis=1)
    return finalize(best, summed, weighted, queries, new_keys, new_values, sinks, heads, kv_heads)


def solution(mesh):
    placed = (
        P(None, ("req", "lend"), None),
        P(None, ("req", "lend"), None),
        P(None, ("req", "lend"), None),
        P(("req", "lend"), None, None),
        P(("req", "lend"), None, None),
        P(("req", "lend"), None, None),
        P(("req", "lend"), None, None),
        P(("req", "lend")),
        P(("req", "lend")),
        P(),
    )
    return jax.shard_map(
        on_device,
        mesh=mesh,
        in_specs=placed,
        out_specs=P(None, ("req", "lend"), None),
        check_vma=False,
    )
```

profile of v0, /device:TPU:1, one launch (start us, length us, event | category | flops | bytes accessed | tf_op | source)
XLA Modules:
  0.0 568.8 jit_solution(11509394585088801762)
XLA Ops:
  1.0 22.0 %all_gather.28 = bf16[1,16,4096]{2,0,1:T(2,128)(2,1)S(1)} all-gather(bf16[1,1,4096]{2,0,1:T(2,128)(2,1)S(1)} %get-tuple-element.23), channel_id=1, replica_groups=mesh['req'=16,'lend'=16] {'lend'}, dimensions={1}, use_global_device_ids=true | all-gather | bytes 139264 | tf_op jit(solution)/shard_map/all_gather | solution.py:135
  23.0 18.8 %all_gather.29 = bf16[1,16,4096]{2,0,1:T(2,128)(2,1)S(1)} all-gather(bf16[1,1,4096]{2,0,1:T(2,128)(2,1)S(1)} %get-tuple-element.23), channel_id=1, replica_groups=mesh['req'=16,'lend'=16] {'req'}, dimensions={1}, use_global_device_ids=true | all-gather | bytes 139264 | tf_op jit(solution)/shard_map/all_gather | solution.py:136
  41.8 20.1 %all_gather.30 = bf16[1,16,4096]{2,0,1:T(2,128)(2,1)S(1)} all-gather(bf16[1,1,4096]{2,0,1:T(2,128)(2,1)S(1)} %get-tuple-element.25), channel_id=1, replica_groups=mesh['req'=16,'lend'=16] {'lend'}, dimensions={1}, use_global_device_ids=true | all-gather | bytes 139264 | tf_op jit(solution)/shard_map/all_gather | solution.py:135
  62.0 17.8 %all_gather.31 = bf16[1,16,4096]{2,0,1:T(2,128)(2,1)S(1)} all-gather(bf16[1,1,4096]{2,0,1:T(2,128)(2,1)S(1)} %get-tuple-element.25), channel_id=1, replica_groups=mesh['req'=16,'lend'=16] {'req'}, dimensions={1}, use_global_device_ids=true | all-gather | bytes 139264 | tf_op jit(solution)/shard_map/all_gather | solution.py:136
  79.8 22.0 %all_gather.24 = bf16[1,16,4096]{2,0,1:T(2,128)(2,1)S(1)} all-gather(bf16[1,1,4096]{2,0,1:T(2,128)(2,1)S(1)} %get-tuple-element.22), channel_id=1, replica_groups=mesh['req'=16,'lend'=16] {'lend'}, dimensions={1}, use_global_device_ids=true | all-gather | bytes 139264 | tf_op jit(solution)/shard_map/all_gather | solution.py:135
  101.8 16.3 %all_gather.25 = bf16[1,16,4096]{2,0,1:T(2,128)(2,1)S(1)} all-gather(bf16[1,1,4096]{2,0,1:T(2,128)(2,1)S(1)} %get-tuple-element.22), channel_id=1, replica_groups=mesh['req'=16,'lend'=16] {'req'}, dimensions={1}, use_global_device_ids=true | all-gather | bytes 139264 | tf_op jit(solution)/shard_map/all_gather | solution.py:136
  118.1 20.1 %all_gather.26 = bf16[1,16,4096]{2,0,1:T(2,128)(2,1)S(1)} all-gather(bf16[1,1,4096]{2,0,1:T(2,128)(2,1)S(1)} %get-tuple-element.24), channel_id=1, replica_groups=mesh['req'=16,'lend'=16] {'lend'}, dimensions={1}, use_global_device_ids=true | all-gather | bytes 139264 | tf_op jit(solution)/shard_map/all_gather | solution.py:135
  138.2 17.8 %all_gather.27 = bf16[1,16,4096]{2,0,1:T(2,128)(2,1)S(1)} all-gather(bf16[1,1,4096]{2,0,1:T(2,128)(2,1)S(1)} %get-tuple-element.24), channel_id=1, replica_groups=mesh['req'=16,'lend'=16] {'req'}, dimensions={1}, use_global_device_ids=true | all-gather | bytes 139264 | tf_op jit(solution)/shard_map/all_gather | solution.py:136
  162.7 8.8 %copy.65 = bf16[48,128,512]{1,2,0:T(8,128)(2,1)} copy(bf16[48,128,512]{2,1,0:T(8,128)(2,1)} %param.15) | data formatting | bytes 12582912 | tf_op args[3]
  185.8 6.5 %bitcast_reduce_fusion.2 = (f32[48,8,8]{2,1,0:T(8,128)}, f32[48,8,128,1,8]{2,4,1,0,3:T(8,128)}) fusion(bf16[48,128,8,64]{1,3,2,0:T(8,128)(2,1)} %bitcast.343, bf16[48,8,8,64]{3,2,1,0:T(8,128)(2,1)} %reshape.1246, pred[48,128]{1,0:T(8,128)(4,1)S(1)} %iota_compare_fusion), kind=kOutput, calls=%fused_computation.43 | convolution fusion | flops 51508224 | bytes 8275968 | tf_op jit(solution)/shard_map/spgae,ptge->spgat/dot_general | solution.py:27
  195.0 6.6 %bitcast_reduce_fusion.3 = (f32[48,8,8]{2,1,0:T(8,128)}, f32[48,8,128,1,8]{2,4,1,0,3:T(8,128)}) fusion(bf16[48,128,8,64]{1,3,2,0:T(8,128)(2,1)} %bitcast.344, bf16[48,8,8,64]{3,2,1,0:T(8,128)(2,1)} %reshape.1243, pred[48,128]{1,0:T(8,128)(4,1)S(1)} %iota_compare_fusion), kind=kOutput, calls=%fused_computation.48 | convolution fusion | flops 51508224 | bytes 8275968 | tf_op jit(solution)/shard_map/spgae,ptge->spgat/dot_general | solution.py:27
  202.7 6.0 %fusion.14 = (f32[48,8,8]{2,1,0:T(8,128)}, f32[48,8,8]{2,1,0:T(8,128)}, f32[48,8,8]{2,1,0:T(8,128)}, f32[48,8,8]{2,1,0:T(8,128)}) fusion(f32[48,8,128,1,8]{2,4,1,0,3:T(8,128)} %get-tuple-element.69, f32[48,8,8]{2,1,0:T(8,128)} %get-tuple-element.68, pred[48,128]{1,0:T(8,128)(4,1)S(1)} %iota_compare_fusion, f32[48,8,8]{2,1,0:T(8,128)} %get-tuple-element.66, ...), kind=kLoop, calls=%fused_computation.52 | loop fusion | flops 4706304 | bytes 6395904 | tf_op jit(solution)/shard_map/reduce_sum | solution.py:34
  225.9 8.6 %copy.64 = bf16[48,128,512]{1,2,0:T(8,128)(2,1)} copy(bf16[48,128,512]{2,1,0:T(8,128)(2,1)} %param.16) | data formatting | bytes 12582912 | tf_op args[4]
  250.9 6.7 %all-to-all-start.3 = ((f32[16,1,64]{2,1,0:T(1,128)}), f32[16,1,64]{2,1,0:T(1,128)S(1)}, u32[]{:S(2)}, u32[]{:S(2)}) async-start(f32[16,1,64]{2,1,0:T(1,128)} %bitcast.22), calls=%async_computation.3 | async-start | bytes 16384 | tf_op jit(solution)/shard_map/all_to_all | solution.py:148
  258.2 5.8 %all-to-all-done.3 = f32[16,1,64]{2,1,0:T(1,128)S(1)} async-done(((f32[16,1,64]{2,1,0:T(1,128)}), f32[16,1,64]{2,1,0:T(1,128)S(1)}, u32[]{:S(2)}, u32[]{:S(2)}) %all-to-all-start.3) | async-done | bytes 4128 | tf_op jit(solution)/shard_map/all_to_all | solution.py:148
  317.3 7.8 %fusion.4 = f32[48,64,64]{2,1,0:T(8,128)} fusion(bf16[48,128,8,64]{1,3,2,0:T(8,128)(2,1)} %bitcast.346, f32[48,8,128,1,8]{2,4,1,0,3:T(8,128)} %get-tuple-element.67, f32[48,64]{1,0:T(8,128)} %subtract_exponential_fusion.2, f32[48,8,8]{2,1,0:T(8,128)} %get-tuple-element.66, pred[48,128]{1,0:T(8,128)(4,1)S(1)} %iota_compare_fusion), kind=kOutput, calls=%fused_computation.29 | convolution fusion | flops 51707904 | bytes 8681472 | tf_op jit(solution)/shard_map/spgat,ptge->spgae/dot_general | solution.py:35
  325.2 17.0 %all-to-all-start.16 = ((f32[16,1,64]{2,1,0:T(1,128)}), f32[16,1,64]{2,1,0:T(1,128)S(1)}, u32[]{:S(2)}, u32[]{:S(2)}) async-start(f32[16,1,64]{2,1,0:T(1,128)} %bitcast.101), calls=%async_computation.16 | async-start | bytes 16384 | tf_op jit(solution)/shard_map/all_to_all | solution.py:144
  342.3 7.0 %all-to-all-done.16 = f32[16,1,64]{2,1,0:T(1,128)S(1)} async-done(((f32[16,1,64]{2,1,0:T(1,128)}), f32[16,1,64]{2,1,0:T(1,128)S(1)}, u32[]{:S(2)}, u32[]{:S(2)}) %all-to-all-start.16) | async-done | bytes 4128 | tf_op jit(solution)/shard_map/all_to_all | solution.py:144
  353.7 7.4 %fusion.3 = f32[48,64,64]{2,1,0:T(8,128)} fusion(bf16[48,128,8,64]{1,3,2,0:T(8,128)(2,1)} %bitcast.347, f32[48,8,128,1,8]{2,4,1,0,3:T(8,128)S(1)} %get-tuple-element.65, f32[48,64]{1,0:T(8,128)S(1)} %subtract_exponential_fusion.1, f32[48,8,8]{2,1,0:T(8,128)} %get-tuple-element.64, pred[48,128]{1,0:T(8,128)(4,1)S(1)} %iota_compare_fusion), kind=kOutput, calls=%fused_computation.27 | convolution fusion | flops 51707904 | bytes 8681472 | tf_op jit(solution)/shard_map/spgat,ptge->spgae/dot_general | solution.py:35
  361.1 7.3 %all-to-all-start.18 = ((f32[16,1,64]{2,1,0:T(1,128)}), f32[16,1,64]{2,1,0:T(1,128)S(1)}, u32[]{:S(2)}, u32[]{:S(2)}) async-start(f32[16,1,64]{2,1,0:T(1,128)} %bitcast.110), calls=%async_computation.18 | async-start | bytes 16384 | tf_op jit(solution)/shard_map/all_to_all | solution.py:144
  368.4 7.0 %all-to-all-done.18 = f32[16,1,64]{2,1,0:T(1,128)S(1)} async-done(((f32[16,1,64]{2,1,0:T(1,128)}), f32[16,1,64]{2,1,0:T(1,128)S(1)}, u32[]{:S(2)}, u32[]{:S(2)}) %all-to-all-start.18) | async-done | bytes 4128 | tf_op jit(solution)/shard_map/all_to_all | solution.py:144
  379.3 7.5 %fusion.2 = f32[48,64,64]{2,1,0:T(8,128)} fusion(bf16[48,128,8,64]{1,3,2,0:T(8,128)(2,1)} %bitcast.348, f32[48,8,128,1,8]{2,4,1,0,3:T(8,128)S(1)} %get-tuple-element.63, f32[48,64]{1,0:T(8,128)S(1)} %subtract_exponential_fusion, f32[48,8,8]{2,1,0:T(8,128)S(1)} %get-tuple-element.62, pred[48,128]{1,0:T(8,128)(4,1)S(1)} %iota_compare_fusion), kind=kOutput, calls=%fused_computation.25 | convolution fusion | flops 51707904 | bytes 8681472 | tf_op jit(solution)/shard_map/spgat,ptge->spgae/dot_general | solution.py:35
  389.9 7.3 %all-to-all-start.20 = ((f32[16,1,64]{2,1,0:T(1,128)}), f32[16,1,64]{2,1,0:T(1,128)S(1)}, u32[]{:S(2)}, u32[]{:S(2)}) async-start(f32[16,1,64]{2,1,0:T(1,128)} %bitcast.119), calls=%async_computation.20 | async-start | bytes 16384 | tf_op jit(solution)/shard_map/all_to_all | solution.py:144
  441.3 7.0 %all-to-all-start.1 = ((f32[16,1,4096]{2,1,0:T(1,128)}), f32[16,1,4096]{2,1,0:T(1,128)S(1)}, u32[]{:S(2)}, u32[]{:S(2)}) async-start(f32[16,1,4096]{2,1,0:T(1,128)} %reshape.1569), calls=%async_computation.1 | async-start | bytes 524288 | tf_op jit(solution)/shard_map/all_to_all | solution.py:150
  458.3 6.8 %all-to-all-start.5 = ((f32[16,1,4096]{2,1,0:T(1,128)}), f32[16,1,4096]{2,1,0:T(1,128)S(1)}, u32[]{:S(2)}, u32[]{:S(2)}) async-start(f32[16,1,4096]{2,1,0:T(1,128)} %reshape.1565), calls=%async_computation.5 | async-start | bytes 524288 | tf_op jit(solution)/shard_map/all_to_all | solution.py:150
  465.2 7.4 %all-to-all-done.5 = f32[16,1,4096]{2,1,0:T(1,128)S(1)} async-done(((f32[16,1,4096]{2,1,0:T(1,128)}), f32[16,1,4096]{2,1,0:T(1,128)S(1)}, u32[]{:S(2)}, u32[]{:S(2)}) %all-to-all-start.5) | async-done | bytes 262176 | tf_op jit(solution)/shard_map/all_to_all | solution.py:150
  476.3 7.5 %all-to-all-done.9 = f32[16,1,4096]{2,1,0:T(1,128)S(1)} async-done(((f32[16,1,4096]{2,1,0:T(1,128)}), f32[16,1,4096]{2,1,0:T(1,128)S(1)}, u32[]{:S(2)}, u32[]{:S(2)}) %all-to-all-start.9) | async-done | bytes 262176 | tf_op jit(solution)/shard_map/all_to_all | solution.py:150
  487.4 7.4 %all-to-all-done.13 = f32[16,1,4096]{2,1,0:T(1,128)S(1)} async-done(((f32[16,1,4096]{2,1,0:T(1,128)}), f32[16,1,4096]{2,1,0:T(1,128)S(1)}, u32[]{:S(2)}, u32[]{:S(2)}) %all-to-all-start.13) | async-done | bytes 262176 | tf_op jit(solution)/shard_map/all_to_all | solution.py:150
  494.8 8.2 %all-to-all-start = ((f32[16,1,4096]{2,1,0:T(1,128)}), f32[16,1,4096]{2,1,0:T(1,128)S(1)}, u32[]{:S(2)}, u32[]{:S(2)}) async-start(f32[16,1,4096]{2,1,0:T(1,128)} %reshape.1571), calls=%async_computation | async-start | bytes 524288 | tf_op jit(solution)/shard_map/all_to_all | solution.py:145
  504.1 10.8 %all-to-all-done = f32[16,1,4096]{2,1,0:T(1,128)S(1)} async-done(((f32[16,1,4096]{2,1,0:T(1,128)}), f32[16,1,4096]{2,1,0:T(1,128)S(1)}, u32[]{:S(2)}, u32[]{:S(2)}) %all-to-all-start) | async-done | bytes 262176 | tf_op jit(solution)/shard_map/all_to_all | solution.py:145
  519.3 10.0 %all-to-all-done.4 = f32[16,1,4096]{2,1,0:T(1,128)S(1)} async-done(((f32[16,1,4096]{2,1,0:T(1,128)}), f32[16,1,4096]{2,1,0:T(1,128)S(1)}, u32[]{:S(2)}, u32[]{:S(2)}) %all-to-all-start.4) | async-done | bytes 262176 | tf_op jit(solution)/shard_map/all_to_all | solution.py:145
  532.8 11.3 %all-to-all-done.8 = f32[16,1,4096]{2,1,0:T(1,128)S(1)} async-done(((f32[16,1,4096]{2,1,0:T(1,128)}), f32[16,1,4096]{2,1,0:T(1,128)S(1)}, u32[]{:S(2)}, u32[]{:S(2)}) %all-to-all-start.8) | async-done | bytes 262176 | tf_op jit(solution)/shard_map/all_to_all | solution.py:145
  (340 shorter events, 218.4 us)
Async XLA Ops:
  0.0 156.0 %copy-start.72 = (s32[48]{0:T(128)S(1)}, s32[48]{0:T(128)}, u32[]{:S(2)}) copy-start(s32[48]{0:T(128)} %param.19) | copy-start | bytes 580
  156.0 65.2 %copy-start.62 = (s32[48]{0:T(128)}, s32[48]{0:T(128)S(1)}, u32[]{:S(2)}) copy-start(s32[48]{0:T(128)S(1)} %get-tuple-element.13) | copy-start | bytes 580
  156.1 66.0 %copy-start.61 = (s32[1024]{0:T(1024)}, s32[1024]{0:T(1024)S(1)}, u32[]{:S(2)}) copy-start(s32[1024]{0:T(1024)S(1)} %pad_clamp_fusion) | copy-start | bytes 12292
  213.3 37.5 %all-to-all-start.17 = ((f32[16,1,64]{2,1,0:T(1,128)}), f32[16,1,64]{2,1,0:T(1,128)}, u32[]{:S(2)}, u32[]{:S(2)}) async-start(f32[16,1,64]{2,1,0:T(1,128)} %bitcast.103), calls=%async_computation.17 | async-start | bytes 16384 | tf_op jit(solution)/shard_map/all_to_all | solution.py:149
  250.9 13.1 %all-to-all-start.3 = ((f32[16,1,64]{2,1,0:T(1,128)}), f32[16,1,64]{2,1,0:T(1,128)S(1)}, u32[]{:S(2)}, u32[]{:S(2)}) async-start(f32[16,1,64]{2,1,0:T(1,128)} %bitcast.22), calls=%async_computation.3 | async-start | bytes 16384 | tf_op jit(solution)/shard_map/all_to_all | solution.py:148
  264.0 9.8 %all-to-all-start.19 = ((f32[16,1,64]{2,1,0:T(1,128)}), f32[16,1,64]{2,1,0:T(1,128)S(1)}, u32[]{:S(2)}, u32[]{:S(2)}) async-start(f32[16,1,64]{2,1,0:T(1,128)} %bitcast.112), calls=%async_computation.19 | async-start | bytes 16384 | tf_op jit(solution)/shard_map/all_to_all | solution.py:149
  273.8 9.9 %all-to-all-start.7 = ((f32[16,1,64]{2,1,0:T(1,128)}), f32[16,1,64]{2,1,0:T(1,128)S(1)}, u32[]{:S(2)}, u32[]{:S(2)}) async-start(f32[16,1,64]{2,1,0:T(1,128)} %bitcast.42), calls=%async_computation.7 | async-start | bytes 16384 | tf_op jit(solution)/shard_map/all_to_all | solution.py:148
  283.7 9.6 %all-to-all-start.21 = ((f32[16,1,64]{2,1,0:T(1,128)}), f32[16,1,64]{2,1,0:T(1,128)S(1)}, u32[]{:S(2)}, u32[]{:S(2)}) async-start(f32[16,1,64]{2,1,0:T(1,128)} %bitcast.121), calls=%async_computation.21 | async-start | bytes 16384 | tf_op jit(solution)/shard_map/all_to_all | solution.py:149
  293.4 10.0 %all-to-all-start.11 = ((f32[16,1,64]{2,1,0:T(1,128)}), f32[16,1,64]{2,1,0:T(1,128)S(1)}, u32[]{:S(2)}, u32[]{:S(2)}) async-start(f32[16,1,64]{2,1,0:T(1,128)} %bitcast.62), calls=%async_computation.11 | async-start | bytes 16384 | tf_op jit(solution)/shard_map/all_to_all | solution.py:148
  303.4 9.8 %all-to-all-start.23 = ((f32[16,1,64]{2,1,0:T(1,128)}), f32[16,1,64]{2,1,0:T(1,128)S(1)}, u32[]{:S(2)}, u32[]{:S(2)}) async-start(f32[16,1,64]{2,1,0:T(1,128)} %bitcast.130), calls=%async_computation.23 | async-start | bytes 16384 | tf_op jit(solution)/shard_map/all_to_all | solution.py:149
  313.8 11.4 %all-to-all-start.15 = ((f32[16,1,64]{2,1,0:T(1,128)}), f32[16,1,64]{2,1,0:T(1,128)S(1)}, u32[]{:S(2)}, u32[]{:S(2)}) async-start(f32[16,1,64]{2,1,0:T(1,128)} %bitcast.82), calls=%async_computation.15 | async-start | bytes 16384 | tf_op jit(solution)/shard_map/all_to_all | solution.py:148
  325.2 24.1 %all-to-all-start.16 = ((f32[16,1,64]{2,1,0:T(1,128)}), f32[16,1,64]{2,1,0:T(1,128)S(1)}, u32[]{:S(2)}, u32[]{:S(2)}) async-start(f32[16,1,64]{2,1,0:T(1,128)} %bitcast.101), calls=%async_computation.16 | async-start | bytes 16384 | tf_op jit(solution)/shard_map/all_to_all | solution.py:144
  349.3 11.8 %all-to-all-start.2 = ((f32[16,1,64]{2,1,0:T(1,128)}), f32[16,1,64]{2,1,0:T(1,128)S(1)}, u32[]{:S(2)}, u32[]{:S(2)}) async-start(f32[16,1,64]{2,1,0:T(1,128)} %bitcast.20), calls=%async_computation.2 | async-start | bytes 16384 | tf_op jit(solution)/shard_map/all_to_all | solution.py:143
  361.1 14.3 %all-to-all-start.18 = ((f32[16,1,64]{2,1,0:T(1,128)}), f32[16,1,64]{2,1,0:T(1,128)S(1)}, u32[]{:S(2)}, u32[]{:S(2)}) async-start(f32[16,1,64]{2,1,0:T(1,128)} %bitcast.110), calls=%async_computation.18 | async-start | bytes 16384 | tf_op jit(solution)/shard_map/all_to_all | solution.py:144
  375.4 14.4 %all-to-all-start.6 = ((f32[16,1,64]{2,1,0:T(1,128)}), f32[16,1,64]{2,1,0:T(1,128)S(1)}, u32[]{:S(2)}, u32[]{:S(2)}) async-start(f32[16,1,64]{2,1,0:T(1,128)} %bitcast.40), calls=%async_computation.6 | async-start | bytes 16384 | tf_op jit(solution)/shard_map/all_to_all | solution.py:143
  389.9 14.3 %all-to-all-start.20 = ((f32[16,1,64]{2,1,0:T(1,128)}), f32[16,1,64]{2,1,0:T(1,128)S(1)}, u32[]{:S(2)}, u32[]{:S(2)}) async-start(f32[16,1,64]{2,1,0:T(1,128)} %bitcast.119), calls=%async_computation.20 | async-start | bytes 16384 | tf_op jit(solution)/shard_map/all_to_all | solution.py:144
  404.8 11.8 %all-to-all-start.10 = ((f32[16,1,64]{2,1,0:T(1,128)}), f32[16,1,64]{2,1,0:T(1,128)S(1)}, u32[]{:S(2)}, u32[]{:S(2)}) async-start(f32[16,1,64]{2,1,0:T(1,128)} %bitcast.60), calls=%async_computation.10 | async-start | bytes 16384 | tf_op jit(solution)/shard_map/all_to_all | solution.py:143
  416.5 12.0 %all-to-all-start.22 = ((f32[16,1,64]{2,1,0:T(1,128)}), f32[16,1,64]{2,1,0:T(1,128)S(1)}, u32[]{:S(2)}, u32[]{:S(2)}) async-start(f32[16,1,64]{2,1,0:T(1,128)} %bitcast.128), calls=%async_computation.22 | async-start | bytes 16384 | tf_op jit(solution)/shard_map/all_to_all | solution.py:144
  428.5 12.1 %all-to-all-start.14 = ((f32[16,1,64]{2,1,0:T(1,128)}), f32[16,1,64]{2,1,0:T(1,128)S(1)}, u32[]{:S(2)}, u32[]{:S(2)}) async-start(f32[16,1,64]{2,1,0:T(1,128)} %bitcast.80), calls=%async_computation.14 | async-start | bytes 16384 | tf_op jit(solution)/shard_map/all_to_all | solution.py:143
  441.3 17.1 %all-to-all-start.1 = ((f32[16,1,4096]{2,1,0:T(1,128)}), f32[16,1,4096]{2,1,0:T(1,128)S(1)}, u32[]{:S(2)}, u32[]{:S(2)}) async-start(f32[16,1,4096]{2,1,0:T(1,128)} %reshape.1569), calls=%async_computation.1 | async-start | bytes 524288 | tf_op jit(solution)/shard_map/all_to_all | solution.py:150
  457.9 61.2 %copy-start.46 = (f32[16,1,64]{2,1,0:T(1,128)S(1)}, f32[16,1,64]{2,1,0:T(1,128)}, u32[]{:S(2)}) copy-start(f32[16,1,64]{2,1,0:T(1,128)} %copy-done.45) | copy-start | bytes 12292
  458.3 14.3 %all-to-all-start.5 = ((f32[16,1,4096]{2,1,0:T(1,128)}), f32[16,1,4096]{2,1,0:T(1,128)S(1)}, u32[]{:S(2)}, u32[]{:S(2)}) async-start(f32[16,1,4096]{2,1,0:T(1,128)} %reshape.1565), calls=%async_computation.5 | async-start | bytes 524288 | tf_op jit(solution)/shard_map/all_to_all | solution.py:150
  465.1 67.6 %copy-start.48 = (f32[16,1,64]{2,1,0:T(1,128)S(1)}, f32[16,1,64]{2,1,0:T(1,128)}, u32[]{:S(2)}) copy-start(f32[16,1,64]{2,1,0:T(1,128)} %copy-done.47) | copy-start | bytes 12292
  465.1 67.6 %copy-start.56 = (f32[16,1,64]{2,1,0:T(1,128)S(1)}, f32[16,1,64]{2,1,0:T(1,128)}, u32[]{:S(2)}) copy-start(f32[16,1,64]{2,1,0:T(1,128)} %copy-done.55) | copy-start | bytes 12292
  472.6 11.1 %all-to-all-start.9 = ((f32[16,1,4096]{2,1,0:T(1,128)}), f32[16,1,4096]{2,1,0:T(1,128)S(1)}, u32[]{:S(2)}, u32[]{:S(2)}) async-start(f32[16,1,4096]{2,1,0:T(1,128)} %reshape.1561), calls=%async_computation.9 | async-start | bytes 524288 | tf_op jit(solution)/shard_map/all_to_all | solution.py:150
  476.2 72.0 %copy-start.50 = (f32[16,1,64]{2,1,0:T(1,128)S(1)}, f32[16,1,64]{2,1,0:T(1,128)}, u32[]{:S(2)}) copy-start(f32[16,1,64]{2,1,0:T(1,128)} %copy-done.49) | copy-start | bytes 12292
  476.2 72.0 %copy-start.58 = (f32[16,1,64]{2,1,0:T(1,128)S(1)}, f32[16,1,64]{2,1,0:T(1,128)}, u32[]{:S(2)}) copy-start(f32[16,1,64]{2,1,0:T(1,128)} %copy-done.57) | copy-start | bytes 12292
  483.7 11.0 %all-to-all-start.13 = ((f32[16,1,4096]{2,1,0:T(1,128)}), f32[16,1,4096]{2,1,0:T(1,128)S(1)}, u32[]{:S(2)}, u32[]{:S(2)}) async-start(f32[16,1,4096]{2,1,0:T(1,128)} %reshape.1557), calls=%async_computation.13 | async-start | bytes 524288 | tf_op jit(solution)/shard_map/all_to_all | solution.py:150
  494.8 20.0 %all-to-all-start = ((f32[16,1,4096]{2,1,0:T(1,128)}), f32[16,1,4096]{2,1,0:T(1,128)S(1)}, u32[]{:S(2)}, u32[]{:S(2)}) async-start(f32[16,1,4096]{2,1,0:T(1,128)} %reshape.1571), calls=%async_computation | async-start | bytes 524288 | tf_op jit(solution)/shard_map/all_to_all | solution.py:145
  514.8 14.5 %all-to-all-start.4 = ((f32[16,1,4096]{2,1,0:T(1,128)}), f32[16,1,4096]{2,1,0:T(1,128)S(1)}, u32[]{:S(2)}, u32[]{:S(2)}) async-start(f32[16,1,4096]{2,1,0:T(1,128)} %reshape.1567), calls=%async_computation.4 | async-start | bytes 524288 | tf_op jit(solution)/shard_map/all_to_all | solution.py:145
  529.3 14.9 %all-to-all-start.8 = ((f32[16,1,4096]{2,1,0:T(1,128)}), f32[16,1,4096]{2,1,0:T(1,128)S(1)}, u32[]{:S(2)}, u32[]{:S(2)}) async-start(f32[16,1,4096]{2,1,0:T(1,128)} %reshape.1563), calls=%async_computation.8 | async-start | bytes 524288 | tf_op jit(solution)/shard_map/all_to_all | solution.py:145
  544.2 18.3 %all-to-all-start.12 = ((f32[16,1,4096]{2,1,0:T(1,128)}), f32[16,1,4096]{2,1,0:T(1,128)}, u32[]{:S(2)}, u32[]{:S(2)}) async-start(f32[16,1,4096]{2,1,0:T(1,128)} %reshape.1559), calls=%async_computation.12 | async-start | bytes 524288 | tf_op jit(solution)/shard_map/all_to_all | solution.py:145
  (66 other events, 1022.8 us)
where the time goes:
time: 576 us; the launch traced here: 569 us
  blocking collectives  155 us (27%)
  starting transfers between devices  127 us (22%)
  waiting for transfers between devices  110 us (19%)
  local copies, waits for them, and re-layouts  75.9 us (13%)
  other arithmetic  54.4 us (9%)
  matrix products  45.6 us (8%)
    all_gather x4, blocking collectives, lent_partials(): row_query = lax.all_gather(query_block, 'lend', axis=1, tiled=True)  84.3 us
    all_gather x4, blocking collectives, lent_partials(): column_query = lax.all_gather(query_block, 'req', axis=1, tiled=True)  70.7 us
    all_to_all x4, starting transfers between devices, lent_partials(): lax.all_to_all(summed[:row_slots], 'lend', split_axis=0, concat_axis=0, t...  36.6 us
    unnamed x166, local copies, waits for them, and re-layouts  35.3 us
    all_to_all x4, waiting for transfers between devices, lent_partials(): lax.all_to_all(weighted[:row_slots], 'lend', split_axis=0, concat_axis=0,...  32.1 us
    dot_general x4, matrix products, page_terms(): jnp.einsum('spgat,ptge->spgae', weights.astype(jnp.bfloat16), value_heads...  27.4 us
    all_to_all x4, waiting for transfers between devices, lent_partials(): lax.all_to_all(weighted[row_slots:], 'req', split_axis=0, concat_axis=0,...  22.3 us
    all_to_all x4, starting transfers between devices, lent_partials(): lax.all_to_all(weighted[row_slots:], 'req', split_axis=0, concat_axis=0,...  20.8 us
  transfers between devices with their start and end apart: 24, of which 18 were waited for; matrix products, arithmetic and copies ran while one was open for 19% of the time, Pallas kernels for 0%

commit v1 on v0

v1 whole, which is shorter than its diff:
```python
import functools

import jax
import jax.numpy as jnp
from jax import lax
from jax.experimental import pallas as pl
from jax.experimental.pallas import tpu as pltpu
from jax.sharding import PartitionSpec as P

FLOOR = -1e30
SCORE_SCALE = 0.125
BF = jnp.bfloat16
F32 = jnp.float32
MESH = pl.DeviceIdType.MESH
GROUPS = 4
MSG = 80


def kernel(
    dims,
    ints,
    qt,
    fresh_kv,
    sinks,
    k_hbm,
    v_hbm,
    ks_hbm,
    vs_hbm,
    out,
    kraw,
    vraw,
    ks,
    vs,
    kd,
    vd,
    q0,
    q1,
    num0,
    num1,
    st0,
    st1,
    stage,
    landed,
    load_sem,
    qsend,
    qrecv,
    psend,
    precv,
):
    n_req, n_lend, pages, chunk, unroll, dunroll = dims
    chunks = pages // chunk
    slots = n_lend + n_req
    req = lax.axis_index("req")
    lend = lax.axis_index("lend")
    qbuf = (q0, q1)
    num = (num0, num1)
    st = (st0, st1)

    def loads(c):
        sl = pl.ds(c * chunk, chunk)
        pairs = ((k_hbm, kraw), (v_hbm, vraw), (ks_hbm, ks), (vs_hbm, vs))
        return [
            pltpu.make_async_copy(src.at[sl], dst.at[sl], load_sem.at[i, c])
            for i, (src, dst) in enumerate(pairs)
        ]

    for c in range(chunks):
        for copy in loads(c):
            copy.start()

    row_peer = lambda k: (req, lax.rem(lend + k, n_lend))
    col_peer = lambda k: (lax.rem(req + k, n_req), lend)

    barrier = pltpu.get_barrier_semaphore()

    def greet(peer):
        def go(k, carry):
            pl.semaphore_signal(barrier, inc=1, device_id=peer(k), device_id_type=MESH)
            return carry

        return go

    lax.fori_loop(1, n_lend, greet(row_peer), 0)
    lax.fori_loop(1, n_req, greet(col_peer), 0)
    for h in range(2):
        qbuf[h][lend] = qt[h]
        qbuf[h][n_lend + req] = qt[h]
    pl.semaphore_wait(barrier, n_lend + n_req - 2)

    def q_row(h, k):
        return pltpu.make_async_remote_copy(
            src_ref=qt.at[h],
            dst_ref=qbuf[h].at[lend],
            send_sem=qsend.at[h, k],
            recv_sem=qrecv.at[h, k],
            device_id=row_peer(k),
            device_id_type=MESH,
        )

    def q_col(h, k):
        return pltpu.make_async_remote_copy(
            src_ref=qt.at[h],
            dst_ref=qbuf[h].at[n_lend + req],
            send_sem=qsend.at[h, n_lend + k],
            recv_sem=qrecv.at[h, n_lend + k],
            device_id=col_peer(k),
            device_id_type=MESH,
        )

    def loop(lo, hi, fn):
        def go(k, carry):
            fn(k)
            return carry

        lax.fori_loop(lo, hi, go, 0)

    for h in range(2):
        loop(1, n_lend, lambda k: q_row(h, k).start())
        loop(1, n_req, lambda k: q_col(h, k).start())

    blk = lax.broadcasted_iota(jnp.int32, (48, 512), 0) % 16
    chan = lax.broadcasted_iota(jnp.int32, (48, 512), 1) // 32
    spread = (blk == chan).astype(F32).astype(BF)

    def dequant(p):
        s = ks[p]
        hi = s.astype(BF)
        rest = s - hi.astype(F32)
        mid = rest.astype(BF)
        low = (rest - mid.astype(F32)).astype(BF)
        parts = jnp.concatenate([hi, mid, low], axis=0)
        wide = lax.dot_general(
            parts, spread, (((0,), (0,)), ((), ())), preferred_element_type=F32
        )
        kd[p] = (kraw[p].astype(F32) * wide).astype(BF)
        vt = vraw[p].T
        sv = jnp.broadcast_to(vs[p][:, None, :], (16, 32, 128)).reshape(512, 128)
        vd[p] = (vt.astype(F32) * sv).astype(BF)

    for c in range(chunks):
        for copy in loads(c):
            copy.wait()

        def some(i, carry):
            for j in range(dunroll):
                dequant(c * chunk + i * dunroll + j)
            return carry

        lax.fori_loop(0, chunk // dunroll, some, 0)

    lane_group = lax.broadcasted_iota(jnp.int32, (64, 128), 1) // 32
    token = lax.broadcasted_iota(jnp.int32, (128, 128), 0)

    def block_diagonal(q):
        zero = jnp.zeros_like(q)
        return jnp.concatenate(
            [jnp.where(lane_group == g, q, zero) for g in range(GROUPS)], axis=0
        )

    def fold(wide):
        x = wide[0:64]
        for g in range(1, GROUPS):
            x = jnp.where(lane_group == g, wide[64 * g : 64 * g + 64], x)
        return x

    def page(p, h):
        slot = ints[0, p]
        fill = ints[2, p]
        qb = block_diagonal(qbuf[h][slot])
        s = jnp.dot(kd[p, :, h * 256 : h * 256 + 256], qb, preferred_element_type=F32)
        s = jnp.where(token < fill, s, FLOOR)
        top = jnp.max(s, axis=0, keepdims=True)
        w = jnp.exp(s - top)
        total = jnp.sum(w, axis=0, keepdims=True)
        wide = jnp.dot(
            vd[p, h * 256 : h * 256 + 256, :], w.astype(BF), preferred_element_type=F32
        )
        return top, total, fold(wide)

    def update(p, h, top, total, x):
        prev = ints[1, p]
        fill = ints[2, p]
        prev_stat = st[h][prev]
        prev_top, prev_total = prev_stat[0:1], prev_stat[1:2]
        best = jnp.maximum(prev_top, top)
        fa = jnp.exp(prev_top - best)
        fb = jnp.where(fill > 0, jnp.exp(top - best), 0.0)
        st[h][p, 0:1, :] = best
        st[h][p, 1:2, :] = prev_total * fa + total * fb
        num[h][p] = num[h][prev] * fa + x * fb

    row16 = lax.broadcasted_iota(jnp.int32, (16, 128), 0)

    def pack(best, total, x):
        bh = best.astype(BF).astype(F32)
        bm = (best - bh).astype(BF).astype(F32)
        bl = best - bh - bm
        th = total.astype(BF).astype(F32)
        tm = total - th
        rows = jnp.zeros((16, 128), F32)
        for i, part in enumerate((bh, bm, bl, th, tm)):
            rows = jnp.where(row16 == i, part, rows)
        return jnp.concatenate([x.astype(BF), rows.astype(BF)], axis=0)

    def unpack(msg):
        x = msg[0:64].astype(F32)
        rows = msg[64:80].astype(F32)
        best = rows[0:1] + rows[1:2] + rows[2:3]
        total = rows[3:4] + rows[4:5]
        return best, total, x

    def partial_copy(h, k, peer):
        return pltpu.make_async_remote_copy(
            src_ref=stage.at[h, k],
            dst_ref=landed.at[h, k],
            send_sem=psend.at[h, k],
            recv_sem=precv.at[h, k],
            device_id=peer,
            device_id_type=MESH,
        )

    def p_row(h, k):
        return partial_copy(h, k, row_peer(k))

    def p_col(h, k):
        return partial_copy(h, n_lend + k, col_peer(k))

    def fill_stage(h, k, slot):
        at = ints[3, slot]
        stat = st[h][at]
        stage[h, k] = pack(stat[0:1], stat[1:2], num[h][at])

    u16 = lax.broadcasted_iota(jnp.int32, (16, 128), 0)
    step16 = (lax.broadcasted_iota(jnp.int32, (16, 128), 1) // 8) % 4

    def fresh(h):
        qb = block_diagonal(qt[h])
        s = jnp.dot(
            fresh_kv[0, :, h * 256 : h * 256 + 256], qb, preferred_element_type=F32
        )
        s = jnp.where(u16 <= step16, s, FLOOR)
        top = jnp.max(s, axis=0, keepdims=True)
        w = jnp.exp(s - top)
        total = jnp.sum(w, axis=0, keepdims=True)
        wide = lax.dot_general(
            fresh_kv[1, :, h * 256 : h * 256 + 256],
            w.astype(BF),
            (((0,), (0,)), ((), ())),
            preferred_element_type=F32,
        )
        return top, total, fold(wide)

    for h in range(2):
        loop(1, n_lend, lambda k: q_row(h, k).wait_recv())
        loop(1, n_req, lambda k: q_col(h, k).wait_recv())
        num[h][pages] = jnp.zeros((64, 128), F32)
        st[h][pages] = jnp.where(
            lax.broadcasted_iota(jnp.int32, (8, 128), 0) == 0, FLOOR, 0.0
        )

        def some_pages(i, carry):
            done = [page(i * unroll + j, h) for j in range(unroll)]
            for j in range(unroll):
                update(i * unroll + j, h, *done[j])
            return carry

        lax.fori_loop(0, pages // unroll, some_pages, 0)

        def send_row(k):
            fill_stage(h, k, lax.rem(lend + k, n_lend))
            p_row(h, k).start()

        def send_col(k):
            fill_stage(h, n_lend + k, n_lend + lax.rem(req + k, n_req))
            p_col(h, k).start()

        loop(1, n_lend, send_row)
        loop(1, n_req, send_col)

    for h in range(2):
        at = ints[3, lend]
        own = st[h][at]
        sink = sinks[h, 0:1, :]
        ftop, ftotal, fx = fresh(h)
        top = jnp.maximum(jnp.maximum(own[0:1], ftop), sink)
        fa = jnp.exp(own[0:1] - top)
        fb = jnp.exp(ftop - top)
        total = own[1:2] * fa + ftotal * fb + jnp.exp(sink - top)
        x = num[h][at] * fa + fx * fb
        loop(1, n_lend, lambda k: p_row(h, k).wait_recv())
        loop(1, n_req, lambda k: p_col(h, k).wait_recv())

        def absorb(k, carry):
            top, total, x = carry
            ktop, ktotal, kx = unpack(landed[h, k])
            best = jnp.maximum(top, ktop)
            fa = jnp.exp(top - best)
            fb = jnp.exp(ktop - best)
            return best, total * fa + ktotal * fb, x * fa + kx * fb

        carry = lax.fori_loop(1, n_lend, absorb, (top, total, x))
        carry = lax.fori_loop(n_lend + 1, slots, absorb, carry)
        out[h] = (carry[2] / carry[1]).astype(BF)

    for h in range(2):
        loop(1, n_lend, lambda k: q_row(h, k).wait_send())
        loop(1, n_req, lambda k: q_col(h, k).wait_send())
        loop(1, n_lend, lambda k: p_row(h, k).wait_send())
        loop(1, n_req, lambda k: p_col(h, k).wait_send())


def on_device(
    queries,
    new_keys,
    new_values,
    key_pool,
    value_pool,
    key_scale,
    value_scale,
    page_request,
    page_fill,
    sinks,
):
    steps = queries.shape[0]
    pages = key_pool.shape[0]
    n_lend = lax.axis_size("lend")
    n_req = lax.axis_size("req")
    req_here = lax.axis_index("req")
    slots = n_lend + n_req
    owner_req = page_request // n_lend
    owner_lend = page_request % n_lend
    slot = jnp.where(owner_req == req_here, owner_lend, n_lend + owner_req)
    ids = jnp.arange(pages, dtype=jnp.int32)
    same = (slot[:, None] == slot[None, :]) & (ids[None, :] < ids[:, None])
    prev = jnp.max(jnp.where(same, ids[None, :], -1), axis=1)
    prev = jnp.where(prev < 0, pages, prev)
    hits = jnp.arange(pages, dtype=jnp.int32)[:, None] == slot[None, :]
    last = jnp.max(jnp.where(hits, ids[None, :], -1), axis=1)
    last = jnp.where(last < 0, pages, last)
    ints = jnp.stack([slot, prev, page_fill, last]).astype(jnp.int32)
    qt = queries.reshape(steps, 2, GROUPS, 8, 64)
    qt = jnp.transpose(qt, (1, 4, 2, 0, 3)).reshape(2, 64, 128)
    qt = qt * jnp.asarray(SCORE_SCALE, BF)
    fresh_kv = jnp.stack([new_keys[:, 0], new_values[:, 0]])
    fresh_kv = jnp.pad(fresh_kv, ((0, 0), (0, 12), (0, 0)))
    sink = jnp.broadcast_to(sinks.reshape(2, 1, GROUPS, 1, 8), (2, 8, GROUPS, steps, 8))
    sink = sink.reshape(2, 8, 128)

    chunk = 6 if pages % 6 == 0 else 4
    dims = (n_req, n_lend, pages, chunk, 12 if pages % 12 == 0 else 4, chunk)
    smem = pl.BlockSpec(memory_space=pltpu.SMEM)
    vmem = pl.BlockSpec(memory_space=pltpu.VMEM)
    hbm = pl.BlockSpec(memory_space=pl.ANY)
    dma = pltpu.SemaphoreType.DMA
    half = pl.pallas_call(
        functools.partial(kernel, dims),
        out_shape=jax.ShapeDtypeStruct((2, 64, 128), BF),
        in_specs=[smem, vmem, vmem, vmem, hbm, hbm, hbm, hbm],
        out_specs=vmem,
        scratch_shapes=[
            pltpu.VMEM((pages, 128, 512), BF),
            pltpu.VMEM((pages, 128, 512), BF),
            pltpu.VMEM((pages, 16, 128), F32),
            pltpu.VMEM((pages, 16, 128), F32),
            pltpu.VMEM((pages, 128, 512), BF),
            pltpu.VMEM((pages, 512, 128), BF),
            pltpu.VMEM((slots, 64, 128), BF),
            pltpu.VMEM((slots, 64, 128), BF),
            pltpu.VMEM((pages + 1, 64, 128), F32),
            pltpu.VMEM((pages + 1, 64, 128), F32),
            pltpu.VMEM((pages + 1, 8, 128), F32),
            pltpu.VMEM((pages + 1, 8, 128), F32),
            pltpu.VMEM((2, slots, MSG, 128), BF),
            pltpu.VMEM((2, slots, MSG, 128), BF),
            dma((4, pages // chunk)),
            dma((2, slots)),
            dma((2, slots)),
            dma((2, slots)),
            dma((2, slots)),
        ],
        compiler_params=pltpu.CompilerParams(
            collective_id=0, has_side_effects=True, vmem_limit_bytes=50 * 2**20
        ),
    )(ints, qt, fresh_kv, sink, key_pool, value_pool, key_scale, value_scale)
    out = half.reshape(2, 64, GROUPS, steps, 8)
    return jnp.transpose(out, (3, 0, 2, 4, 1)).reshape(steps, 1, 4096)


def solution(mesh):
    placed = (
        P(None, ("req", "lend"), None),
        P(None, ("req", "lend"), None),
        P(None, ("req", "lend"), None),
        P(("req", "lend"), None, None),
        P(("req", "lend"), None, None),
        P(("req", "lend"), None, None),
        P(("req", "lend"), None, None),
        P(("req", "lend")),
        P(("req", "lend")),
        P(),
    )
    return jax.shard_map(
        on_device,
        mesh=mesh,
        in_specs=placed,
        out_specs=P(None, ("req", "lend"), None),
        check_vma=False,
    )
```

time: 576 us -> 53 us (0.09); the launches traced: 569 us -> 52.7 us
  blocking collectives: 155 us -> 0 us
  starting transfers between devices: 127 us -> 0 us
  waiting for transfers between devices: 110 us -> 0 us
  local copies, waits for them, and re-layouts: 75.9 us -> 3.93 us
  other arithmetic: 54.4 us -> 3.68 us
  matrix products: 45.6 us -> 0 us
  Pallas kernels: 0 us -> 45 us
    all_gather x8 -> x0, blocking collectives: 155 us -> none  [the longest x4 84.3 us: lent_partials(): row_query = lax.all_gather(query_block, 'lend', axis=1, tiled=True)]
    all_to_all x24 -> x0, starting transfers between devices: 127 us -> none  [the longest x4 36.6 us: lent_partials(): lax.all_to_all(summed[:row_slots], 'lend', split_axis=0, concat_axis=0, t...]
    all_to_all x24 -> x0, waiting for transfers between devices: 110 us -> none  [the longest x4 32.1 us: lent_partials(): lax.all_to_all(weighted[:row_slots], 'lend', split_axis=0, concat_axis=0,...]
    dot_general x10 -> x0, matrix products: 45.6 us -> none  [the longest x4 27.4 us: page_terms(): jnp.einsum('spgat,ptge->spgae', weights.astype(jnp.bfloat16), value_heads...]
    pallas_call x0 -> x1, Pallas kernels: none -> 45 us  [on_device(): pl.pallas_call(functools.partial(kernel, dims), out_shape=jax.ShapeDtypeS...]
    unnamed x166 -> x4, local copies, waits for them, and re-layouts: 35.3 us -> 1.99 us
    scatter-add x8 -> x0, other arithmetic: 15 us -> none  [the longest x4 11.7 us: gather_slots(): jax.ops.segment_sum(page_numer * factor[..., None], slot, num_segments=co...]
    another operation x23 -> x0, local copies, waits for them, and re-layouts: 14 us -> none
  transfers between devices with their start and end apart: 24 -> 0, of which waited for: 18 -> 0; matrix products, arithmetic and copies ran while one was open for 19% -> 0% of each run, Pallas kernels for 0% -> 0%
where the time goes in v1:
time: 53 us; the launch traced here: 52.7 us
  Pallas kernels  45 us (85%)
  local copies, waits for them, and re-layouts  3.93 us (7%)
  other arithmetic  3.68 us (7%)
    pallas_call x1, Pallas kernels, on_device(): pl.pallas_call(functools.partial(kernel, dims), out_shape=jax.ShapeDtypeS...  45 us
    unnamed x4, local copies, waits for them, and re-layouts  1.99 us
    another operation x2, other arithmetic, on_device(): ints = jnp.stack([slot, prev, page_fill, last]).astype(jnp.int32)  1.34 us

profile of v1, /device:TPU:1, one launch (start us, length us, event | category | flops | bytes accessed | tf_op | source)
XLA Modules:
  0.0 52.7 jit_solution(18331984301817258320)
XLA Ops:
  0.0 0.7 %compare_select_fusion.2 = s32[48]{0:T(128)S(1)} fusion(s32[48]{0:T(128)} %param.17, s32[]{:T(128)S(6)} %axis_index.15), kind=kLoop, calls=%fused_computation.14 | loop fusion | flops 1056 | bytes 388 | tf_op jit(solution)/shard_map/jit(_where)/select_n | solution.py:332
  0.7 0.2 select_reduce_fusion.1
  0.9 0.7 %fusion.4 = s32[1,48]{1,0:T(1,128)S(1)} fusion(s32[]{:T(128)S(6)} %axis_index.15, s32[48]{0:T(128)} %param.17), kind=kLoop, calls=%fused_computation.19 | loop fusion | flops 1056 | bytes 388 | tf_op jit(solution)/shard_map/stack | solution.py:340
  1.5 0.7 %pad_add_fusion.ints = s32[4,48]{1,0:T(4,128)S(1)} fusion(s32[1,48]{1,0:T(1,128)S(1)} %get-tuple-element.7, s32[1,48]{1,0:T(1,128)} %bitcast.23, s32[1,48]{1,0:T(1,128)S(1)} %get-tuple-element.8, s32[1,48]{1,0:T(1,128)S(1)} %fusion.4), kind=kLoop, calls=%fused_computation.12 | loop fusion | flops 576 | bytes 1536 | tf_op jit(solution)/shard_map/stack | solution.py:340
  2.2 0.8 %broadcast_multiply_fusion = bf16[4,1,4096]{2,0,1:T(4,128)(2,1)S(1)} fusion(bf16[4,1,4096]{2,0,1:T(4,128)(2,1)} %param.10), kind=kLoop, calls=%fused_computation.9 | loop fusion | flops 16384 | bytes 65536 | tf_op jit(solution)/shard_map/mul | solution.py:343
  3.0 0.1 mul.14
  3.1 0.1 copy.21.qt
  3.2 0.7 %fusion.2.fresh_kv = bf16[2,16,512]{2,1,0:T(8,128)(2,1)S(1)} fusion(bf16[1,4,512]{2,1,0:T(4,128)(2,1)} %bitcast.21, bf16[1,4,512]{2,1,0:T(4,128)(2,1)} %bitcast.22), kind=kLoop, calls=%fused_computation.3 | loop fusion | flops 114688 | bytes 40960 | tf_op jit(solution)/shard_map/stack | solution.py:344
  3.9 0.7 %broadcast_in_dim.40 = f32[2,4,8]{2,1,0:T(4,128)S(1)} reshape(f32[64]{0:T(128)} %param.19) | data formatting | bytes 512 | tf_op jit(solution)/shard_map/broadcast_in_dim | solution.py:346
  4.7 0.1 broadcast_in_dim.42
  4.8 0.0 copy-start
  4.8 1.0 %copy-done = f32[48,16,128]{2,1,0:T(8,128)S(1)} copy-done((f32[48,16,128]{2,1,0:T(8,128)S(1)}, f32[48,16,128]{2,1,0:T(8,128)}, u32[]{:S(2)}) %copy-start) | copy-done | bytes 393240
  5.8 0.0 copy-start.1
  5.8 1.0 %copy-done.1 = f32[48,16,128]{2,1,0:T(8,128)S(1)} copy-done((f32[48,16,128]{2,1,0:T(8,128)S(1)}, f32[48,16,128]{2,1,0:T(8,128)}, u32[]{:S(2)}) %copy-start.1) | copy-done | bytes 393240
  6.8 45.0 %shard_map.100 = bf16[2,64,128]{2,1,0:T(8,128)(2,1)S(1)} custom-call(s32[4,48]{1,0:T(4,128)S(1)} %pad_add_fusion.ints, bf16[2,64,128]{2,1,0:T(8,128)(2,1)S(1)} %copy.21.qt, bf16[2,16,512]{2,1,0:T(8,128)(2,1)S(1)} %fusion.2.fresh_kv, f32[2,8,128]{2,1,0:T(8,128)S(1)} %broadcast_in_dim.43.sinks, bf16[48,128,512]{2,1,0:T(8,128)(2,1)} %k_hbm.1, ...), custom_call_target="tpu_custom_call" | custom-call | tf_op jit(solution)/shard_map/pallas_call | solution.py:355
  51.8 0.1 copy.22
  51.9 0.7 %reshape.39 = bf16[4,1,4096]{2,0,1:T(4,128)(2,1)} reshape(bf16[4,2,4,8,64]{4,3,2,1,0:T(8,128)(2,1)S(1)} %copy.23) | data formatting | bytes 65536 | tf_op jit(solution)/shard_map/reshape | solution.py:386
  (5 shorter events, 0.0 us)
Async XLA Ops:
  4.8 1.0 %copy-start = (f32[48,16,128]{2,1,0:T(8,128)S(1)}, f32[48,16,128]{2,1,0:T(8,128)}, u32[]{:S(2)}) copy-start(f32[48,16,128]{2,1,0:T(8,128)} %ks_hbm.1) | copy-start | bytes 1179652
  5.8 1.0 %copy-start.1 = (f32[48,16,128]{2,1,0:T(8,128)S(1)}, f32[48,16,128]{2,1,0:T(8,128)}, u32[]{:S(2)}) copy-start(f32[48,16,128]{2,1,0:T(8,128)} %vs_hbm.1) | copy-start | bytes 1179652

commit v2 on v1

v2 whole, which is shorter than its diff:
```python
import functools

import jax
import jax.numpy as jnp
from jax import lax
from jax.experimental import pallas as pl
from jax.experimental.pallas import tpu as pltpu
from jax.sharding import PartitionSpec as P

FLOOR = -1e30
SCORE_SCALE = 0.125
BF = jnp.bfloat16
F32 = jnp.float32
MESH = pl.DeviceIdType.MESH
GROUPS = 4
MSG = 80


def kernel(
    dims,
    q_hbm,
    nk_hbm,
    nv_hbm,
    k_hbm,
    v_hbm,
    ks_hbm,
    vs_hbm,
    req_hbm,
    fill_hbm,
    sink_hbm,
    out,
    kraw,
    vraw,
    ks,
    vs,
    kd,
    vd,
    q0,
    q1,
    num0,
    num1,
    st0,
    st1,
    stage,
    landed,
    q_raw,
    q_rows,
    qt,
    fresh_raw,
    fresh_f32,
    req_vec,
    fill_vec,
    req_s,
    sink_s,
    slot_sub,
    int_vec,
    ints,
    load_sem,
    small_sem,
    qsend,
    qrecv,
    psend,
    precv,
):
    n_req, n_lend, pages, chunk, unroll, dunroll = dims
    chunks = pages // chunk
    slots = n_lend + n_req
    req = lax.axis_index("req")
    lend = lax.axis_index("lend")
    qbuf = (q0, q1)
    num = (num0, num1)
    st = (st0, st1)

    def loads(c):
        sl = pl.ds(c * chunk, chunk)
        pairs = ((k_hbm, kraw), (v_hbm, vraw), (ks_hbm, ks), (vs_hbm, vs))
        return [
            pltpu.make_async_copy(src.at[sl], dst.at[sl], load_sem.at[i, c])
            for i, (src, dst) in enumerate(pairs)
        ]

    smalls = [
        pltpu.make_async_copy(src, dst, small_sem.at[i])
        for i, (src, dst) in enumerate(
            (
                (q_hbm, q_raw),
                (req_hbm, req_vec),
                (req_hbm, req_s),
                (fill_hbm, fill_vec),
                (sink_hbm, sink_s),
                (nk_hbm, fresh_raw.at[0]),
                (nv_hbm, fresh_raw.at[1]),
            )
        )
    ]
    for copy in smalls:
        copy.start()
    for c in range(chunks):
        for copy in loads(c):
            copy.start()

    ring_n = n_lend // 2
    ring = lend // 2
    core = lend % 2
    sibling = (req, 2 * ring + 1 - core)
    row_lend = lambda k: 2 * lax.rem(ring + k, ring_n) + core
    cross_lend = lambda k: 2 * lax.rem(ring + k, ring_n) + 1 - core
    from_lend = lambda k: 2 * lax.rem(ring + ring_n - k, ring_n) + core
    row_peer = lambda k: (req, row_lend(k))
    col_peer = lambda k: (lax.rem(req + k, n_req), lend)

    def loop(lo, hi, fn):
        def go(k, carry):
            fn(k)
            return carry

        lax.fori_loop(lo, hi, go, 0)

    barrier = pltpu.get_barrier_semaphore()

    def greet(peer):
        pl.semaphore_signal(barrier, inc=1, device_id=peer, device_id_type=MESH)

    greet(sibling)
    loop(1, ring_n, lambda k: greet(row_peer(k)))
    loop(1, n_req, lambda k: greet(col_peer(k)))

    smalls[0].wait()
    for j in range(32):
        h, g, ap = j // 16, (j // 4) % 4, j % 4
        tile = q_raw[:, j * 128 : j * 128 + 128].astype(F32) * SCORE_SCALE
        q_rows[pl.ds(h * 64 + g * 16 + ap, 4, stride=4), :] = tile
    turned = q_rows[...].T
    low_lanes = lax.broadcasted_iota(jnp.int32, (64, 128), 1) < 64
    even, odd = turned[0:64], turned[64:128]
    qt[0] = jnp.where(low_lanes, even, pltpu.roll(odd, 64, 1)).astype(BF)
    qt[1] = jnp.where(low_lanes, pltpu.roll(even, 64, 1), odd).astype(BF)
    for h in range(2):
        qbuf[h][lend] = qt[h]
    pl.semaphore_wait(barrier, ring_n + n_req - 1)

    def q_copy(src, h, at, slot, peer):
        return pltpu.make_async_remote_copy(
            src_ref=src,
            dst_ref=qbuf[h].at[slot],
            send_sem=qsend.at[h, at],
            recv_sem=qrecv.at[h, at],
            device_id=peer,
            device_id_type=MESH,
        )

    def q_row(h, k):
        return q_copy(qt.at[h], h, k, lend, row_peer(k))

    def q_own(h):
        return q_copy(qt.at[h], h, ring_n, lend, sibling)

    def q_pass(h, k):
        slot = from_lend(k)
        return q_copy(qbuf[h].at[slot], h, ring_n + k, slot, sibling)

    def q_col(h, k):
        return q_copy(qt.at[h], h, n_lend + k, n_lend + req, col_peer(k))

    for h in range(2):
        loop(1, ring_n, lambda k: q_row(h, k).start())
        loop(1, n_req, lambda k: q_col(h, k).start())
        q_own(h).start()

    def forward(h):
        def go(k):
            q_row(h, k).wait_recv()
            q_pass(h, k).start()

        loop(1, ring_n, go)

    for copy in smalls[1:]:
        copy.wait()

    def slot_of(request):
        owner_req = request // n_lend
        return jnp.where(owner_req == req, request % n_lend, n_lend + owner_req)

    def spread_slot(p):
        slot_sub[pl.ds(p, 1), :] = jnp.full((1, 128), slot_of(req_s[0, p]), jnp.int32)

    loop(0, pages, spread_slot)
    slot_lane = slot_of(req_vec[...])
    sub = slot_sub[...]
    page_sub = lax.broadcasted_iota(jnp.int32, (pages, pages), 0)
    page_lane = lax.broadcasted_iota(jnp.int32, (pages, pages), 1)
    same = (sub[:, 0:pages] == slot_lane) & (page_sub < page_lane)
    prev = jnp.max(jnp.where(same, page_sub, -1), axis=0, keepdims=True)
    hit = sub == lax.broadcasted_iota(jnp.int32, (pages, 128), 1)
    last = jnp.where(hit, lax.broadcasted_iota(jnp.int32, (pages, 128), 0), -1)
    last = jnp.max(last, axis=0, keepdims=True)
    int_vec[0:1, 0:pages] = slot_lane
    int_vec[1:2, 0:pages] = jnp.where(prev < 0, pages, prev)
    int_vec[2:3, 0:pages] = fill_vec[...]
    int_vec[3:4, :] = jnp.where(last < 0, pages, last)
    ints_copy = pltpu.make_async_copy(int_vec, ints, small_sem.at[7])
    ints_copy.start()

    fresh_f32[...] = jnp.zeros((2, 16, 512), F32)
    for i in range(2):
        fresh_f32[i, 0:4, :] = fresh_raw[i].astype(F32)
    lane = lax.broadcasted_iota(jnp.int32, (1, 128), 1)
    lane_head = (lane // 16) % 4 * 8 + (lane % 4) * 2 + lane // 64
    sink_rows = []
    for h in range(2):
        x = jnp.zeros((1, 128), F32)
        for i in range(32):
            x = jnp.where(lane_head == i, sink_s[0, h * 32 + i], x)
        sink_rows.append(x)

    blk = lax.broadcasted_iota(jnp.int32, (48, 512), 0) % 16
    chan = lax.broadcasted_iota(jnp.int32, (48, 512), 1) // 32
    spread = (blk == chan).astype(F32).astype(BF)

    def dequant(p):
        s = ks[p]
        hi = s.astype(BF)
        rest = s - hi.astype(F32)
        mid = rest.astype(BF)
        low = (rest - mid.astype(F32)).astype(BF)
        parts = jnp.concatenate([hi, mid, low], axis=0)
        wide = lax.dot_general(
            parts, spread, (((0,), (0,)), ((), ())), preferred_element_type=F32
        )
        kd[p] = (kraw[p].astype(F32) * wide).astype(BF)
        vt = vraw[p].T
        sv = jnp.broadcast_to(vs[p][:, None, :], (16, 32, 128)).reshape(512, 128)
        vd[p] = (vt.astype(F32) * sv).astype(BF)

    for c in range(chunks):
        for copy in loads(c):
            copy.wait()

        def some(i, carry):
            for j in range(dunroll):
                dequant(c * chunk + i * dunroll + j)
            return carry

        lax.fori_loop(0, chunk // dunroll, some, 0)
        if c == chunks - 2:
            forward(0)

    ints_copy.wait()
    lane_group = lax.broadcasted_iota(jnp.int32, (64, 128), 1) // 16 % 4
    token = lax.broadcasted_iota(jnp.int32, (128, 128), 0)

    def block_diagonal(q):
        zero = jnp.zeros_like(q)
        return jnp.concatenate(
            [jnp.where(lane_group == g, q, zero) for g in range(GROUPS)], axis=0
        )

    def fold(wide):
        x = wide[0:64]
        for g in range(1, GROUPS):
            x = jnp.where(lane_group == g, wide[64 * g : 64 * g + 64], x)
        return x

    def page(p, h):
        slot = ints[0, p]
        fill = ints[2, p]
        qb = block_diagonal(qbuf[h][slot])
        s = jnp.dot(kd[p, :, h * 256 : h * 256 + 256], qb, preferred_element_type=F32)
        s = jnp.where(token < fill, s, FLOOR)
        top = jnp.max(s, axis=0, keepdims=True)
        w = jnp.exp(s - top)
        total = jnp.sum(w, axis=0, keepdims=True)
        wide = jnp.dot(
            vd[p, h * 256 : h * 256 + 256, :], w.astype(BF), preferred_element_type=F32
        )
        return top, total, fold(wide)

    def update(p, h, top, total, x):
        prev = ints[1, p]
        fill = ints[2, p]
        prev_stat = st[h][prev]
        prev_top, prev_total = prev_stat[0:1], prev_stat[1:2]
        best = jnp.maximum(prev_top, top)
        fa = jnp.exp(prev_top - best)
        fb = jnp.where(fill > 0, jnp.exp(top - best), 0.0)
        st[h][p, 0:1, :] = best
        st[h][p, 1:2, :] = prev_total * fa + total * fb
        num[h][p] = num[h][prev] * fa + x * fb

    row16 = lax.broadcasted_iota(jnp.int32, (16, 128), 0)

    def pack(best, total, x):
        bh = best.astype(BF).astype(F32)
        bm = (best - bh).astype(BF).astype(F32)
        bl = best - bh - bm
        th = total.astype(BF).astype(F32)
        tm = total - th
        rows = jnp.zeros((16, 128), F32)
        for i, part in enumerate((bh, bm, bl, th, tm)):
            rows = jnp.where(row16 == i, part, rows)
        return jnp.concatenate([x.astype(BF), rows.astype(BF)], axis=0)

    def unpack(msg):
        x = msg[0:64].astype(F32)
        rows = msg[64:80].astype(F32)
        best = rows[0:1] + rows[1:2] + rows[2:3]
        total = rows[3:4] + rows[4:5]
        return best, total, x

    def partial_copy(h, k, peer):
        return pltpu.make_async_remote_copy(
            src_ref=stage.at[h, k],
            dst_ref=landed.at[h, k],
            send_sem=psend.at[h, k],
            recv_sem=precv.at[h, k],
            device_id=peer,
            device_id_type=MESH,
        )

    def p_row(h, k):
        return partial_copy(h, k, row_peer(k))

    def p_cross(h, k):
        return partial_copy(h, ring_n + k, sibling)

    def p_col(h, k):
        return partial_copy(h, n_lend + k, col_peer(k))

    def mine(h, slot):
        at = ints[3, slot]
        stat = st[h][at]
        return stat[0:1], stat[1:2], num[h][at]

    def merge(one, two):
        best = jnp.maximum(one[0], two[0])
        fa = jnp.exp(one[0] - best)
        fb = jnp.exp(two[0] - best)
        return best, one[1] * fa + two[1] * fb, one[2] * fa + two[2] * fb

    def send_cross(h):
        def go(k):
            stage[h, ring_n + k] = pack(*mine(h, cross_lend(k)))
            p_cross(h, k).start()

        loop(0, ring_n, go)

    def send_col(h):
        def go(k):
            stage[h, n_lend + k] = pack(*mine(h, n_lend + lax.rem(req + k, n_req)))
            p_col(h, k).start()

        loop(1, n_req, go)

    def send_row(h):
        def go(k):
            p_cross(h, k).wait_recv()
            both = merge(mine(h, row_lend(k)), unpack(landed[h, ring_n + k]))
            stage[h, k] = pack(*both)
            p_row(h, k).start()

        loop(1, ring_n, go)

    u16 = lax.broadcasted_iota(jnp.int32, (16, 128), 0)
    step16 = (lax.broadcasted_iota(jnp.int32, (16, 128), 1) // 4) % 4

    def fresh(h):
        qb = block_diagonal(qt[h])
        s = jnp.dot(
            fresh_f32[0, :, h * 256 : h * 256 + 256].astype(BF), qb, preferred_element_type=F32
        )
        s = jnp.where(u16 <= step16, s, FLOOR)
        top = jnp.max(s, axis=0, keepdims=True)
        w = jnp.exp(s - top)
        total = jnp.sum(w, axis=0, keepdims=True)
        wide = lax.dot_general(
            fresh_f32[1, :, h * 256 : h * 256 + 256].astype(BF),
            w.astype(BF),
            (((0,), (0,)), ((), ())),
            preferred_element_type=F32,
        )
        return top, total, fold(wide)

    def attend(h, lo, hi):
        def some_pages(i, carry):
            done = [page(i * unroll + j, h) for j in range(unroll)]
            for j in range(unroll):
                update(i * unroll + j, h, *done[j])
            return carry

        lax.fori_loop(lo, hi, some_pages, 0)

    rounds = pages // unroll
    for h in range(2):
        num[h][pages] = jnp.zeros((64, 128), F32)
        st[h][pages] = jnp.where(
            lax.broadcasted_iota(jnp.int32, (8, 128), 0) == 0, FLOOR, 0.0
        )
    for h in range(2):
        loop(0, ring_n, lambda k: q_copy(qt.at[h], h, ring_n + k, lend, sibling).wait_recv())
        loop(1, n_req, lambda k: q_col(h, k).wait_recv())
        attend(h, 0, rounds // 2)
        if h == 0:
            forward(1)
        else:
            send_row(0)
        attend(h, rounds // 2, rounds)
        send_cross(h)
        send_col(h)

    bases = []
    for h in range(2):
        new = fresh(h)
        sink = sink_rows[h]
        base = merge(new, mine(h, lend))
        top = jnp.maximum(base[0], sink)
        fa = jnp.exp(base[0] - top)
        bases.append((top, base[1] * fa + jnp.exp(sink - top), base[2] * fa))
    send_row(1)

    for h in range(2):
        p_cross(h, 0).wait_recv()
        loop(1, n_req, lambda k: p_col(h, k).wait_recv())
        loop(1, ring_n, lambda k: p_row(h, k).wait_recv())

        def absorb(k, carry):
            return merge(carry, unpack(landed[h, k]))

        carry = merge(bases[h], unpack(landed[h, ring_n]))
        carry = lax.fori_loop(n_lend + 1, slots, absorb, carry)
        carry = lax.fori_loop(1, ring_n, absorb, carry)
        out[h] = (carry[2] / carry[1]).astype(BF)

    for h in range(2):
        loop(1, ring_n, lambda k: q_row(h, k).wait_send())
        q_own(h).wait_send()
        loop(1, ring_n, lambda k: q_pass(h, k).wait_send())
        loop(1, n_req, lambda k: q_col(h, k).wait_send())
        loop(1, ring_n, lambda k: p_row(h, k).wait_send())
        loop(0, ring_n, lambda k: p_cross(h, k).wait_send())
        loop(1, n_req, lambda k: p_col(h, k).wait_send())


def on_device(
    queries,
    new_keys,
    new_values,
    key_pool,
    value_pool,
    key_scale,
    value_scale,
    page_request,
    page_fill,
    sinks,
):
    steps = queries.shape[0]
    pages = key_pool.shape[0]
    n_lend = lax.axis_size("lend")
    n_req = lax.axis_size("req")
    slots = n_lend + n_req
    chunk = 6 if pages % 6 == 0 else 4
    dims = (n_req, n_lend, pages, chunk, 24 if pages % 48 == 0 else 4, chunk)
    vmem = pl.BlockSpec(memory_space=pltpu.VMEM)
    hbm = pl.BlockSpec(memory_space=pltpu.MemorySpace.HBM)
    dma = pltpu.SemaphoreType.DMA
    half = pl.pallas_call(
        functools.partial(kernel, dims),
        out_shape=jax.ShapeDtypeStruct((2, 64, 128), BF),
        in_specs=[hbm] * 10,
        out_specs=vmem,
        scratch_shapes=[
            pltpu.VMEM((pages, 128, 512), BF),
            pltpu.VMEM((pages, 128, 512), BF),
            pltpu.VMEM((pages, 16, 128), F32),
            pltpu.VMEM((pages, 16, 128), F32),
            pltpu.VMEM((pages, 128, 512), BF),
            pltpu.VMEM((pages, 512, 128), BF),
            pltpu.VMEM((slots, 64, 128), BF),
            pltpu.VMEM((slots, 64, 128), BF),
            pltpu.VMEM((pages + 1, 64, 128), F32),
            pltpu.VMEM((pages + 1, 64, 128), F32),
            pltpu.VMEM((pages + 1, 8, 128), F32),
            pltpu.VMEM((pages + 1, 8, 128), F32),
            pltpu.VMEM((2, slots, MSG, 128), BF),
            pltpu.VMEM((2, slots, MSG, 128), BF),
            pltpu.VMEM((4, 4096), BF),
            pltpu.VMEM((128, 128), F32),
            pltpu.VMEM((2, 64, 128), BF),
            pltpu.VMEM((2, 4, 512), BF),
            pltpu.VMEM((2, 16, 512), F32),
            pltpu.VMEM((1, pages), jnp.int32),
            pltpu.VMEM((1, pages), jnp.int32),
            pltpu.SMEM((1, pages), jnp.int32),
            pltpu.SMEM((1, 64), F32),
            pltpu.VMEM((pages, 128), jnp.int32),
            pltpu.VMEM((8, 128), jnp.int32),
            pltpu.SMEM((8, 128), jnp.int32),
            dma((4, pages // chunk)),
            dma((8,)),
            dma((2, slots)),
            dma((2, slots)),
            dma((2, slots)),
            dma((2, slots)),
        ],
        compiler_params=pltpu.CompilerParams(
            collective_id=0, has_side_effects=True, vmem_limit_bytes=63 * 2**20
        ),
    )(
        queries.reshape(steps, 4096),
        new_keys.reshape(steps, 512),
        new_values.reshape(steps, 512),
        key_pool,
        value_pool,
        key_scale,
        value_scale,
        page_request.reshape(1, pages),
        page_fill.reshape(1, pages),
        sinks.reshape(1, 64),
    )
    out = half.reshape(2, 64, 2, GROUPS, steps, 4)
    return jnp.transpose(out, (4, 0, 3, 5, 2, 1)).reshape(steps, 1, 4096)


def solution(mesh):
    placed = (
        P(None, ("req", "lend"), None),
        P(None, ("req", "lend"), None),
        P(None, ("req", "lend"), None),
        P(("req", "lend"), None, None),
        P(("req", "lend"), None, None),
        P(("req", "lend"), None, None),
        P(("req", "lend"), None, None),
        P(("req", "lend")),
        P(("req", "lend")),
        P(),
    )
    return jax.shard_map(
        on_device,
        mesh=mesh,
        in_specs=placed,
        out_specs=P(None, ("req", "lend"), None),
        check_vma=False,
    )
```

time: 53 us -> 38.9 us (0.73)
  Pallas kernels: 45 us -> 37 us
  other arithmetic: 3.68 us -> 0 us
  local copies, waits for them, and re-layouts: 3.93 us -> 1.67 us
    pallas_call x1, Pallas kernels: 45 us -> 37 us  [on_device(): pl.pallas_call(functools.partial(kernel, dims), out_shape=jax.ShapeDtypeS...]
    another operation x3 -> x0, other arithmetic: 2.06 us -> none  [the longest x2 1.34 us: on_device(): ints = jnp.stack([slot, prev, page_fill, last]).astype(jnp.int32)]
    unnamed x4 -> x0, local copies, waits for them, and re-layouts: 1.99 us -> none
    broadcast_in_dim x4 -> x0, local copies, waits for them, and re-layouts: 0.85 us -> none  [on_device(): jnp.broadcast_to(sinks.reshape(2, 1, GROUPS, 1, 8), (2, 8, GROUPS, steps,...]
    mul x1 -> x0, other arithmetic: 0.78 us -> none  [on_device(): qt = qt * jnp.asarray(SCORE_SCALE, BF)]
    pallas_call x1, local copies, waits for them, and re-layouts: 0.12 us -> 0.87 us  [on_device(): pl.pallas_call(functools.partial(kernel, dims), out_shape=jax.ShapeDtypeS...]
    select_n x2 -> x0, other arithmetic: 0.67 us -> none  [the longest x1 0.67 us: on_device(): slot = jnp.where(owner_req == req_here, owner_lend, n_lend + owner_req)]
where the time goes in v2:
time: 38.9 us; the launch traced here: 38.7 us
  Pallas kernels  37 us (95%)
  local copies, waits for them, and re-layouts  1.67 us (4%)
    pallas_call x1, Pallas kernels, on_device(): pl.pallas_call(functools.partial(kernel, dims), out_shape=jax.ShapeDtypeS...  37 us
    pallas_call x1, local copies, waits for them, and re-layouts, on_device(): pl.pallas_call(functools.partial(kernel, dims), out_shape=jax.ShapeDtypeS...  0.87 us

profile of v2, /device:TPU:1, one launch (start us, length us, event | category | flops | bytes accessed | tf_op | source)
XLA Modules:
  0.0 38.7 jit_solution(15495003787816055328)
XLA Ops:
  0.0 37.0 %shard_map.100 = bf16[2,64,128]{2,1,0:T(8,128)(2,1)} custom-call(bf16[4,4096]{1,0:T(4,128)(2,1)} %bitcast.10, bf16[4,512]{1,0:T(4,128)(2,1)} %bitcast.11, bf16[4,512]{1,0:T(4,128)(2,1)} %bitcast.12, bf16[48,128,512]{2,1,0:T(8,128)(2,1)} %k_hbm.1, bf16[48,128,512]{2,1,0:T(8,128)(2,1)} %v_hbm.1, f32[48,16,128]{2,1,0:T(8,128)} %ks_hbm.1, ...), custom_call_target="tpu_custom_call" | custom-call | tf_op jit(solution)/shard_map/pallas_call | solution.py:465
  37.1 0.9 %copy.13 = bf16[2,64,128]{1,2,0:T(8,128)(2,1)S(1)} copy(bf16[2,64,128]{2,1,0:T(8,128)(2,1)} %shard_map.100) | data formatting | bytes 65536 | tf_op jit(solution)/shard_map/pallas_call | solution.py:465
  37.9 0.1 copy.14
  38.0 0.7 %reshape.31 = bf16[4,1,4096]{2,0,1:T(4,128)(2,1)} reshape(bf16[4,2,4,4,2,64]{5,4,3,2,1,0:T(2,128)(2,1)S(1)} %copy.14) | data formatting | bytes 65536 | tf_op jit(solution)/shard_map/reshape | solution.py:520

commit v3 on v2

--- a/solution.py
+++ b/solution.py
@@ -93,12 +93,6 @@
             )
         )
     ]
-    for copy in smalls:
-        copy.start()
-    for c in range(chunks):
-        for copy in loads(c):
-            copy.start()
-
     ring_n = n_lend // 2
     ring = lend // 2
     core = lend % 2
@@ -107,7 +101,20 @@
     cross_lend = lambda k: 2 * lax.rem(ring + k, ring_n) + 1 - core
     from_lend = lambda k: 2 * lax.rem(ring + ring_n - k, ring_n) + core
     row_peer = lambda k: (req, row_lend(k))
-    col_peer = lambda k: (lax.rem(req + k, n_req), lend)
+    xs = 4 if n_req % 4 == 0 else n_req
+    ys = n_req // xs
+
+    def col_req(k):
+        y = lax.rem(req // xs + k // xs, ys)
+        return y * xs + lax.rem(req % xs + k % xs, xs)
+
+    col_peer = lambda k: (col_req(k), lend)
+    cross_peer = lambda k: (req, cross_lend(k))
+    hops = lambda k: min(k, ring_n - k)
+    near_first = sorted(range(1, ring_n), key=hops)
+    far = [k for k in near_first if hops(k) >= 3]
+    far_q = (far, [])
+    far_p = ([], far)
 
     def loop(lo, hi, fn):
         def go(k, carry):
@@ -124,6 +131,44 @@
     greet(sibling)
     loop(1, ring_n, lambda k: greet(row_peer(k)))
     loop(1, n_req, lambda k: greet(col_peer(k)))
+    for k in far:
+        greet(cross_peer(k))
+
+    for copy in smalls:
+        copy.start()
+    for c in range(chunks):
+        for copy in loads(c):
+            copy.start()
+
+    blk = lax.broadcasted_iota(jnp.int32, (48, 512), 0) % 16
+    chan = lax.broadcasted_iota(jnp.int32, (48, 512), 1) // 32
+    spread = (blk == chan).astype(F32).astype(BF)
+
+    def dequant(p):
+        s = ks[p]
+        hi = s.astype(BF)
+        rest = s - hi.astype(F32)
+        mid = rest.astype(BF)
+        low = (rest - mid.astype(F32)).astype(BF)
+        parts = jnp.concatenate([hi, mid, low], axis=0)
+        wide = lax.dot_general(
+            parts, spread, (((0,), (0,)), ((), ())), preferred_element_type=F32
+        )
+        kd[p] = (kraw[p].astype(F32) * wide).astype(BF)
+        vt = vraw[p].T
+        sv = jnp.broadcast_to(vs[p][:, None, :], (16, 32, 128)).reshape(512, 128)
+        vd[p] = (vt.astype(F32) * sv).astype(BF)
+
+    def dequant_chunk(c):
+        for copy in loads(c):
+            copy.wait()
+
+        def some(i, carry):
+            for j in range(dunroll):
+                dequant(c * chunk + i * dunroll + j)
+            return carry
+
+        lax.fori_loop(0, chunk // dunroll, some, 0)
 
     smalls[0].wait()
     for j in range(32):
@@ -137,7 +182,10 @@
     qt[1] = jnp.where(low_lanes, pltpu.roll(even, 64, 1), odd).astype(BF)
     for h in range(2):
         qbuf[h][lend] = qt[h]
-    pl.semaphore_wait(barrier, ring_n + n_req - 1)
+    early = min(3, chunks - 1)
+    for c in range(early):
+        dequant_chunk(c)
+    pl.semaphore_wait(barrier, ring_n + n_req - 1 + len(far))
 
     def q_copy(src, h, at, slot, peer):
         return pltpu.make_async_remote_copy(
@@ -155,6 +203,9 @@
     def q_own(h):
         return q_copy(qt.at[h], h, ring_n, lend, sibling)
 
+    def q_cross(h, k):
+        return q_copy(qt.at[h], h, ring_n + k, lend, cross_peer(k))
+
     def q_pass(h, k):
         slot = from_lend(k)
         return q_copy(qbuf[h].at[slot], h, ring_n + k, slot, sibling)
@@ -163,16 +214,18 @@
         return q_copy(qt.at[h], h, n_lend + k, n_lend + req, col_peer(k))
 
     for h in range(2):
-        loop(1, ring_n, lambda k: q_row(h, k).start())
-        loop(1, n_req, lambda k: q_col(h, k).start())
+        for k in reversed(near_first):
+            q_row(h, k).start()
+            if k in far_q[h]:
+                q_cross(h, k).start()
+        loop(1, n_req, lambda k: q_col(h, n_req - k).start())
         q_own(h).start()
 
     def forward(h):
-        def go(k):
+        for k in near_first:
             q_row(h, k).wait_recv()
-            q_pass(h, k).start()
-
-        loop(1, ring_n, go)
+            if k not in far_q[h]:
+                q_pass(h, k).start()
 
     for copy in smalls[1:]:
         copy.wait()
@@ -213,39 +266,6 @@
             x = jnp.where(lane_head == i, sink_s[0, h * 32 + i], x)
         sink_rows.append(x)
 
-    blk = lax.broadcasted_iota(jnp.int32, (48, 512), 0) % 16
-    chan = lax.broadcasted_iota(jnp.int32, (48, 512), 1) // 32
-    spread = (blk == chan).astype(F32).astype(BF)
-
-    def dequant(p):
-        s = ks[p]
-        hi = s.astype(BF)
-        rest = s - hi.astype(F32)
-        mid = rest.astype(BF)
-        low = (rest - mid.astype(F32)).astype(BF)
-        parts = jnp.concatenate([hi, mid, low], axis=0)
-        wide = lax.dot_general(
-            parts, spread, (((0,), (0,)), ((), ())), preferred_element_type=F32
-        )
-        kd[p] = (kraw[p].astype(F32) * wide).astype(BF)
-        vt = vraw[p].T
-        sv = jnp.broadcast_to(vs[p][:, None, :], (16, 32, 128)).reshape(512, 128)
-        vd[p] = (vt.astype(F32) * sv).astype(BF)
-
-    for c in range(chunks):
-        for copy in loads(c):
-            copy.wait()
-
-        def some(i, carry):
-            for j in range(dunroll):
-                dequant(c * chunk + i * dunroll + j)
-            return carry
-
-        lax.fori_loop(0, chunk // dunroll, some, 0)
-        if c == chunks - 2:
-            forward(0)
-
-    ints_copy.wait()
     lane_group = lax.broadcasted_iota(jnp.int32, (64, 128), 1) // 16 % 4
     token = lax.broadcasted_iota(jnp.int32, (128, 128), 0)
 
@@ -261,6 +281,31 @@
             x = jnp.where(lane_group == g, wide[64 * g : 64 * g + 64], x)
         return x
 
+    u16 = lax.broadcasted_iota(jnp.int32, (16, 128), 0)
+    step16 = (lax.broadcasted_iota(jnp.int32, (16, 128), 1) // 4) % 4
+
+    def fresh(h):
+        qb = block_diagonal(qt[h])
+        s = jnp.dot(
+            fresh_f32[0, :, h * 256 : h * 256 + 256].astype(BF), qb, preferred_element_type=F32
+        )
+        s = jnp.where(u16 <= step16, s, FLOOR)
+        top = jnp.max(s, axis=0, keepdims=True)
+        w = jnp.exp(s - top)
+        total = jnp.sum(w, axis=0, keepdims=True)
+        wide = lax.dot_general(
+            fresh_f32[1, :, h * 256 : h * 256 + 256].astype(BF),
+            w.astype(BF),
+            (((0,), (0,)), ((), ())),
+            preferred_element_type=F32,
+        )
+        return top, total, fold(wide)
+
+    news = [fresh(h) for h in range(2)]
+    for c in range(early, chunks):
+        dequant_chunk(c)
+    forward(0)
+    ints_copy.wait()
     def page(p, h):
         slot = ints[0, p]
         fill = ints[2, p]
@@ -337,48 +382,33 @@
         fb = jnp.exp(two[0] - best)
         return best, one[1] * fa + two[1] * fb, one[2] * fa + two[2] * fb
 
+    def p_far(h, k):
+        return partial_copy(h, ring_n + k, cross_peer(k))
+
     def send_cross(h):
-        def go(k):
+        for k in reversed([0] + near_first):
             stage[h, ring_n + k] = pack(*mine(h, cross_lend(k)))
-            p_cross(h, k).start()
-
-        loop(0, ring_n, go)
+            if k in far_p[h]:
+                p_far(h, k).start()
+                stage[h, k] = pack(*mine(h, row_lend(k)))
+                p_row(h, k).start()
+            else:
+                p_cross(h, k).start()
 
     def send_col(h):
         def go(k):
-            stage[h, n_lend + k] = pack(*mine(h, n_lend + lax.rem(req + k, n_req)))
+            stage[h, n_lend + k] = pack(*mine(h, n_lend + col_req(k)))
             p_col(h, k).start()
 
         loop(1, n_req, go)
 
     def send_row(h):
-        def go(k):
-            p_cross(h, k).wait_recv()
-            both = merge(mine(h, row_lend(k)), unpack(landed[h, ring_n + k]))
-            stage[h, k] = pack(*both)
-            p_row(h, k).start()
-
-        loop(1, ring_n, go)
-
-    u16 = lax.broadcasted_iota(jnp.int32, (16, 128), 0)
-    step16 = (lax.broadcasted_iota(jnp.int32, (16, 128), 1) // 4) % 4
-
-    def fresh(h):
-        qb = block_diagonal(qt[h])
-        s = jnp.dot(
-            fresh_f32[0, :, h * 256 : h * 256 + 256].astype(BF), qb, preferred_element_type=F32
-        )
-        s = jnp.where(u16 <= step16, s, FLOOR)
-        top = jnp.max(s, axis=0, keepdims=True)
-        w = jnp.exp(s - top)
-        total = jnp.sum(w, axis=0, keepdims=True)
-        wide = lax.dot_general(
-            fresh_f32[1, :, h * 256 : h * 256 + 256].astype(BF),
-            w.astype(BF),
-            (((0,), (0,)), ((), ())),
-            preferred_element_type=F32,
-        )
-        return top, total, fold(wide)
+        for k in reversed(near_first):
+            if k not in far_p[h]:
+                p_cross(h, k).wait_recv()
+                both = merge(mine(h, row_lend(k)), unpack(landed[h, ring_n + k]))
+                stage[h, k] = pack(*both)
+                p_row(h, k).start()
 
     def attend(h, lo, hi):
         def some_pages(i, carry):
@@ -407,36 +437,52 @@
         send_cross(h)
         send_col(h)
 
-    bases = []
-    for h in range(2):
-        new = fresh(h)
+    send_row(1)
+
+    halves = []
+    for h in range(2):
         sink = sink_rows[h]
-        base = merge(new, mine(h, lend))
+        base = merge(news[h], mine(h, lend))
         top = jnp.maximum(base[0], sink)
         fa = jnp.exp(base[0] - top)
-        bases.append((top, base[1] * fa + jnp.exp(sink - top), base[2] * fa))
-    send_row(1)
-
-    for h in range(2):
+        carry = (top, base[1] * fa + jnp.exp(sink - top), base[2] * fa)
+
+        def absorb(at, carry):
+            return merge(carry, unpack(landed[h, at]))
+
         p_cross(h, 0).wait_recv()
-        loop(1, n_req, lambda k: p_col(h, k).wait_recv())
-        loop(1, ring_n, lambda k: p_row(h, k).wait_recv())
-
-        def absorb(k, carry):
-            return merge(carry, unpack(landed[h, k]))
-
-        carry = merge(bases[h], unpack(landed[h, ring_n]))
-        carry = lax.fori_loop(n_lend + 1, slots, absorb, carry)
-        carry = lax.fori_loop(1, ring_n, absorb, carry)
-        out[h] = (carry[2] / carry[1]).astype(BF)
-
-    for h in range(2):
-        loop(1, ring_n, lambda k: q_row(h, k).wait_send())
+        carry = absorb(ring_n, carry)
+
+        def absorb_col(k, carry):
+            p_col(h, k).wait_recv()
+            return absorb(n_lend + k, carry)
+
+        carry = lax.fori_loop(1, n_req, absorb_col, carry)
+        for k in near_first:
+            p_row(h, k).wait_recv()
+            carry = absorb(k, carry)
+            if k in far_p[h]:
+                p_far(h, k).wait_recv()
+                carry = absorb(ring_n + k, carry)
+        halves.append(carry[2] / carry[1])
+
+    even = jnp.where(low_lanes, halves[0], pltpu.roll(halves[1], 64, 1))
+    odd = jnp.where(low_lanes, pltpu.roll(halves[0], 64, 1), halves[1])
+    q_rows[...] = jnp.concatenate([even, odd], axis=0).T
+    for j in range(32):
+        h, g, ap = j // 16, (j // 4) % 4, j % 4
+        tile = q_rows[pl.ds(h * 64 + g * 16 + ap, 4, stride=4), :]
+        out[:, j * 128 : j * 128 + 128] = tile.astype(BF)
+
+    for h in range(2):
         q_own(h).wait_send()
-        loop(1, ring_n, lambda k: q_pass(h, k).wait_send())
+        for k in near_first:
+            q_row(h, k).wait_send()
+            (q_cross if k in far_q[h] else q_pass)(h, k).wait_send()
+            p_row(h, k).wait_send()
+            (p_far if k in far_p[h] else p_cross)(h, k).wait_send()
+        p_cross(h, 0).wait_send()
         loop(1, n_req, lambda k: q_col(h, k).wait_send())
-        loop(1, ring_n, lambda k: p_row(h, k).wait_send())
-        loop(0, ring_n, lambda k: p_cross(h, k).wait_send())
         loop(1, n_req, lambda k: p_col(h, k).wait_send())
 
 
@@ -462,9 +508,9 @@
     vmem = pl.BlockSpec(memory_space=pltpu.VMEM)
     hbm = pl.BlockSpec(memory_space=pltpu.MemorySpace.HBM)
     dma = pltpu.SemaphoreType.DMA
-    half = pl.pallas_call(
+    out = pl.pallas_call(
         functools.partial(kernel, dims),
-        out_shape=jax.ShapeDtypeStruct((2, 64, 128), BF),
+        out_shape=jax.ShapeDtypeStruct((4, 4096), BF),
         in_specs=[hbm] * 10,
         out_specs=vmem,
         scratch_shapes=[
@@ -516,8 +562,7 @@
         page_fill.reshape(1, pages),
         sinks.reshape(1, 64),
     )
-    out = half.reshape(2, 64, 2, GROUPS, steps, 4)
-    return jnp.transpose(out, (4, 0, 3, 5, 2, 1)).reshape(steps, 1, 4096)
+    return out.reshape(steps, 1, 4096)
 
 
 def solution(mesh):

time: 38.9 us -> 41.4 us (1.064)
  Pallas kernels: 37 us -> 39.9 us
    pallas_call x1, Pallas kernels: 37 us -> 39.9 us  [on_device(): pl.pallas_call(functools.partial(kernel, dims), out_shape=jax.ShapeDtypeS...]
    unnamed x0 -> x1, local copies, waits for them, and re-layouts: none -> 1.39 us
    pallas_call x1 -> x0, local copies, waits for them, and re-layouts: 0.87 us -> none  [on_device(): pl.pallas_call(functools.partial(kernel, dims), out_shape=jax.ShapeDtypeS...]
    reshape x1 -> x0, local copies, waits for them, and re-layouts: 0.73 us -> none  [on_device(): return jnp.transpose(out, (4, 0, 3, 5, 2, 1)).reshape(steps, 1, 4096)]
where the time goes in v3:
time: 41.4 us; the launch traced here: 41.3 us
  Pallas kernels  39.9 us (96%)
  local copies, waits for them, and re-layouts  1.39 us (3%)
    pallas_call x1, Pallas kernels, on_device(): pl.pallas_call(functools.partial(kernel, dims), out_shape=jax.ShapeDtypeS...  39.9 us
    unnamed x1, local copies, waits for them, and re-layouts  1.39 us

profile of v3, /device:TPU:1, one launch (start us, length us, event | category | flops | bytes accessed | tf_op | source)
XLA Modules:
  0.0 41.3 jit_solution(12291484119366627397)
XLA Ops:
  0.0 39.9 %shard_map.100 = bf16[4,4096]{1,0:T(4,128)(2,1)} custom-call(bf16[4,4096]{1,0:T(4,128)(2,1)} %bitcast.8, bf16[4,512]{1,0:T(4,128)(2,1)} %bitcast.9, bf16[4,512]{1,0:T(4,128)(2,1)} %bitcast.10, bf16[48,128,512]{2,1,0:T(8,128)(2,1)} %k_hbm.1, bf16[48,128,512]{2,1,0:T(8,128)(2,1)} %v_hbm.1, f32[48,16,128]{2,1,0:T(8,128)} %ks_hbm.1, f32[48,16,128]{2,1,0:T(8,128)} %vs_hbm.1, ...), custom_call_target="tpu_custom_call" | custom-call | tf_op jit(solution)/shard_map/pallas_call | solution.py:511
  39.9 1.4 %copy.12 = bf16[4,1,4096]{2,0,1:T(4,128)(2,1)} copy(bf16[4,1,4096]{2,0,1:T(4,128)(2,1)} %bitcast.7) | data formatting | bytes 65536

commit v4 on v3

--- a/solution.py
+++ b/solution.py
@@ -109,12 +109,8 @@
         return y * xs + lax.rem(req % xs + k % xs, xs)
 
     col_peer = lambda k: (col_req(k), lend)
-    cross_peer = lambda k: (req, cross_lend(k))
     hops = lambda k: min(k, ring_n - k)
     near_first = sorted(range(1, ring_n), key=hops)
-    far = [k for k in near_first if hops(k) >= 3]
-    far_q = (far, [])
-    far_p = ([], far)
 
     def loop(lo, hi, fn):
         def go(k, carry):
@@ -131,8 +127,6 @@
     greet(sibling)
     loop(1, ring_n, lambda k: greet(row_peer(k)))
     loop(1, n_req, lambda k: greet(col_peer(k)))
-    for k in far:
-        greet(cross_peer(k))
 
     for copy in smalls:
         copy.start()
@@ -182,10 +176,7 @@
     qt[1] = jnp.where(low_lanes, pltpu.roll(even, 64, 1), odd).astype(BF)
     for h in range(2):
         qbuf[h][lend] = qt[h]
-    early = min(3, chunks - 1)
-    for c in range(early):
-        dequant_chunk(c)
-    pl.semaphore_wait(barrier, ring_n + n_req - 1 + len(far))
+    pl.semaphore_wait(barrier, ring_n + n_req - 1)
 
     def q_copy(src, h, at, slot, peer):
         return pltpu.make_async_remote_copy(
@@ -203,9 +194,6 @@
     def q_own(h):
         return q_copy(qt.at[h], h, ring_n, lend, sibling)
 
-    def q_cross(h, k):
-        return q_copy(qt.at[h], h, ring_n + k, lend, cross_peer(k))
-
     def q_pass(h, k):
         slot = from_lend(k)
         return q_copy(qbuf[h].at[slot], h, ring_n + k, slot, sibling)
@@ -216,16 +204,13 @@
     for h in range(2):
         for k in reversed(near_first):
             q_row(h, k).start()
-            if k in far_q[h]:
-                q_cross(h, k).start()
         loop(1, n_req, lambda k: q_col(h, n_req - k).start())
         q_own(h).start()
 
     def forward(h):
         for k in near_first:
             q_row(h, k).wait_recv()
-            if k not in far_q[h]:
-                q_pass(h, k).start()
+            q_pass(h, k).start()
 
     for copy in smalls[1:]:
         copy.wait()
@@ -302,7 +287,7 @@
         return top, total, fold(wide)
 
     news = [fresh(h) for h in range(2)]
-    for c in range(early, chunks):
+    for c in range(chunks):
         dequant_chunk(c)
     forward(0)
     ints_copy.wait()
@@ -382,32 +367,41 @@
         fb = jnp.exp(two[0] - best)
         return best, one[1] * fa + two[1] * fb, one[2] * fa + two[2] * fb
 
-    def p_far(h, k):
-        return partial_copy(h, ring_n + k, cross_peer(k))
-
     def send_cross(h):
-        for k in reversed([0] + near_first):
-            stage[h, ring_n + k] = pack(*mine(h, cross_lend(k)))
-            if k in far_p[h]:
-                p_far(h, k).start()
-                stage[h, k] = pack(*mine(h, row_lend(k)))
-                p_row(h, k).start()
-            else:
+        order = list(reversed([0] + near_first))
+        for at in range(0, ring_n, 4):
+            some = order[at : at + 4]
+            packed = [pack(*mine(h, cross_lend(k))) for k in some]
+            for k, msg in zip(some, packed):
+                stage[h, ring_n + k] = msg
+            for k in some:
                 p_cross(h, k).start()
 
+    col_group = 5 if (n_req - 1) % 5 == 0 else 1
+
     def send_col(h):
-        def go(k):
-            stage[h, n_lend + k] = pack(*mine(h, n_lend + col_req(k)))
-            p_col(h, k).start()
-
-        loop(1, n_req, go)
+        def go(i):
+            some = [1 + i * col_group + j for j in range(col_group)]
+            packed = [pack(*mine(h, n_lend + col_req(k))) for k in some]
+            for k, msg in zip(some, packed):
+                stage[h, n_lend + k] = msg
+            for k in some:
+                p_col(h, k).start()
+
+        loop(0, (n_req - 1) // col_group, go)
 
     def send_row(h):
-        for k in reversed(near_first):
-            if k not in far_p[h]:
+        order = list(reversed(near_first))
+        for some in (order[:3], order[3:]):
+            for k in some:
                 p_cross(h, k).wait_recv()
-                both = merge(mine(h, row_lend(k)), unpack(landed[h, ring_n + k]))
-                stage[h, k] = pack(*both)
+            packed = [
+                pack(*merge(mine(h, row_lend(k)), unpack(landed[h, ring_n + k])))
+                for k in some
+            ]
+            for k, msg in zip(some, packed):
+                stage[h, k] = msg
+            for k in some:
                 p_row(h, k).start()
 
     def attend(h, lo, hi):
@@ -458,12 +452,18 @@
             return absorb(n_lend + k, carry)
 
         carry = lax.fori_loop(1, n_req, absorb_col, carry)
+        q_own(h).wait_send()
+        p_cross(h, 0).wait_send()
+        loop(1, n_req, lambda k: q_col(h, k).wait_send())
+        loop(1, n_req, lambda k: p_col(h, k).wait_send())
+        for k in near_first:
+            q_row(h, k).wait_send()
+            q_pass(h, k).wait_send()
+            p_cross(h, k).wait_send()
+            p_row(h, k).wait_send()
         for k in near_first:
             p_row(h, k).wait_recv()
             carry = absorb(k, carry)
-            if k in far_p[h]:
-                p_far(h, k).wait_recv()
-                carry = absorb(ring_n + k, carry)
         halves.append(carry[2] / carry[1])
 
     even = jnp.where(low_lanes, halves[0], pltpu.roll(halves[1], 64, 1))
@@ -473,17 +473,6 @@
         h, g, ap = j // 16, (j // 4) % 4, j % 4
         tile = q_rows[pl.ds(h * 64 + g * 16 + ap, 4, stride=4), :]
         out[:, j * 128 : j * 128 + 128] = tile.astype(BF)
-
-    for h in range(2):
-        q_own(h).wait_send()
-        for k in near_first:
-            q_row(h, k).wait_send()
-            (q_cross if k in far_q[h] else q_pass)(h, k).wait_send()
-            p_row(h, k).wait_send()
-            (p_far if k in far_p[h] else p_cross)(h, k).wait_send()
-        p_cross(h, 0).wait_send()
-        loop(1, n_req, lambda k: q_col(h, k).wait_send())
-        loop(1, n_req, lambda k: p_col(h, k).wait_send())
 
 
 def on_device(

time: 41.4 us -> 38 us (0.918)
  Pallas kernels: 39.9 us -> 36.5 us
    pallas_call x1, Pallas kernels: 39.9 us -> 36.5 us  [on_device(): pl.pallas_call(functools.partial(kernel, dims), out_shape=jax.ShapeDtypeS...]
where the time goes in v4:
time: 38 us; the launch traced here: 37.9 us
  Pallas kernels  36.5 us (96%)
  local copies, waits for them, and re-layouts  1.39 us (4%)
    pallas_call x1, Pallas kernels, on_device(): pl.pallas_call(functools.partial(kernel, dims), out_shape=jax.ShapeDtypeS...  36.5 us
    unnamed x1, local copies, waits for them, and re-layouts  1.39 us

profile of v4, /device:TPU:1, one launch (start us, length us, event | category | flops | bytes accessed | tf_op | source)
XLA Modules:
  0.0 37.9 jit_solution(15985767161314243023)
XLA Ops:
  0.0 36.5 %shard_map.100 = bf16[4,4096]{1,0:T(4,128)(2,1)} custom-call(bf16[4,4096]{1,0:T(4,128)(2,1)} %bitcast.8, bf16[4,512]{1,0:T(4,128)(2,1)} %bitcast.9, bf16[4,512]{1,0:T(4,128)(2,1)} %bitcast.10, bf16[48,128,512]{2,1,0:T(8,128)(2,1)} %k_hbm.1, bf16[48,128,512]{2,1,0:T(8,128)(2,1)} %v_hbm.1, f32[48,16,128]{2,1,0:T(8,128)} %ks_hbm.1, f32[48,16,128]{2,1,0:T(8,128)} %vs_hbm.1, ...), custom_call_target="tpu_custom_call" | custom-call | tf_op jit(solution)/shard_map/pallas_call | solution.py:500
  36.5 1.4 %copy.12 = bf16[4,1,4096]{2,0,1:T(4,128)(2,1)} copy(bf16[4,1,4096]{2,0,1:T(4,128)(2,1)} %bitcast.7) | data formatting | bytes 65536
